TPU v7x, 32 devices: a whole 2x2x4 slice. The times are simulated.
32 devices in a mesh: dp: 8 (over z, y), tensor: 4 (over x, core).
Axes of the slice: x: 2, y: 2, z: 4, core: 2. Of those that a mesh axis runs over, the one named last changes fastest.
Arguments:
- tokens: bfloat16 [16384, 1024], P(('dp', 'tensor')), may hold values from -6 to 6
- w_in: bfloat16 [1024, 3, 1024], P(None, None, 'tensor'), may hold values from -0.1875 to 0.1875
- conv_kernel: bfloat16 [3, 1024], P(None, 'tensor'), may hold values from -3.5 to 3.5
- w_out: bfloat16 [1024, 1024], P('tensor'), may hold values from -0.1875 to 0.1875
- w_gate: bfloat16 [1024, 4608], P(None, 'tensor'), may hold values from -0.1875 to 0.1875
- w_up: bfloat16 [1024, 4608], P(None, 'tensor'), may hold values from -0.1875 to 0.1875
- w_down: bfloat16 [4608, 1024], P('tensor'), may hold values from -0.09375 to 0.09375
- gain_mix: float32 [1024], replicated, may hold values from 0.25 to 1.75
- gain_mlp: float32 [1024], replicated, may hold values from 0.25 to 1.75
- cotangent: bfloat16 [16384, 1024], P(('dp', 'tensor')), may hold values from -6 to 6
Outputs:
- result: float32 [16384, 1024], P(('dp', 'tensor'))
- grad_tokens: float32 [16384, 1024], P(('dp', 'tensor'))
- grad_w_in: float32 [1024, 3, 1024], P(None, None, 'tensor')
- grad_kernel: float32 [3, 1024], P(None, 'tensor')
- grad_w_out: float32 [1024, 1024], P('tensor')
- grad_w_gate: float32 [1024, 4608], P(None, 'tensor')
- grad_w_up: float32 [1024, 4608], P(None, 'tensor')
- grad_w_down: float32 [4608, 1024], P('tensor')
- grad_gain_mix: float32 [1024], replicated
- grad_gain_mlp: float32 [1024], replicated
All inputs are finite; a program needn't handle non-finite values.
Results may differ from a plain program's by a relative error of at most 0.011.
Values may be sent and summed in bfloat16 or wider, within the bound.
A program may use at most 192 MiB of HBM per device.

v0:
```python
import jax
import jax.numpy as jnp
from jax import lax
from jax.sharding import PartitionSpec as P

LEN = 1024


EPSILON = 1e-05


def rms_scale(values):
    scale = lax.rsqrt(jnp.mean(values * values, axis=-1, keepdims=True) + EPSILON)
    return (values * scale, scale)


def norm_back(grad_norm, unit, scale, gain):
    weighted = grad_norm * gain
    return scale * (weighted - unit * jnp.mean(weighted * unit, axis=-1, keepdims=True))


def shift_down(values, shift_by):
    return jnp.pad(values, ((0, 0), (shift_by, 0), (0, 0)))[:, : values.shape[1], :]


def shift_up(values, shift_by):
    return jnp.pad(values, ((0, 0), (0, shift_by), (0, 0)))[:, shift_by:, :]


def dot_first(left, right):
    return lax.dot_general(
        left, right, (((0,), (0,)), ((), ())), preferred_element_type=jnp.float32
    )


def dot_last(left, right):
    return lax.dot_general(
        left, right, (((1,), (1,)), ((), ())), preferred_element_type=jnp.float32
    )


def shards(tokens, w_in, conv_kernel, w_out, w_gate, w_up, w_down, gain_mix, gain_mlp, cotangent):
    model_width = tokens.shape[1]
    channels = conv_kernel.shape[1]
    in_flat = w_in.reshape(model_width, 3 * channels)
    taps = conv_kernel.astype(jnp.float32)
    inputs = tokens.astype(jnp.float32)
    unit_one, scale_one = rms_scale(inputs)
    normed_one = lax.all_gather(
        (unit_one * gain_mix).astype(jnp.bfloat16), "tensor", axis=0, tiled=True
    )
    projected = jnp.dot(normed_one, in_flat, preferred_element_type=jnp.float32)
    b_part = projected[:, :channels]
    c_part = projected[:, channels : 2 * channels]
    x_part = projected[:, 2 * channels :]
    seq_gated = (b_part * x_part).reshape(-1, LEN, channels)
    back_one = shift_down(seq_gated, 1)
    back_two = shift_down(seq_gated, 2)
    convolved = (taps[0] * back_two + taps[1] * back_one + taps[2] * seq_gated).reshape(
        -1, channels
    )
    mixed_low = (c_part * convolved).astype(jnp.bfloat16)
    resid = inputs + lax.psum_scatter(
        jnp.dot(mixed_low, w_out, preferred_element_type=jnp.float32),
        "tensor",
        scatter_dimension=0,
        tiled=True,
    )
    unit_two, scale_two = rms_scale(resid)
    normed_two = lax.all_gather(
        (unit_two * gain_mlp).astype(jnp.bfloat16), "tensor", axis=0, tiled=True
    )
    gate_pre = jnp.dot(normed_two, w_gate, preferred_element_type=jnp.float32)
    up_pre = jnp.dot(normed_two, w_up, preferred_element_type=jnp.float32)
    sig_gate = jax.nn.sigmoid(gate_pre)
    activated = gate_pre * sig_gate
    hidden_low = (activated * up_pre).astype(jnp.bfloat16)
    result = resid + lax.psum_scatter(
        jnp.dot(hidden_low, w_down, preferred_element_type=jnp.float32).astype(jnp.bfloat16),
        "tensor",
        scatter_dimension=0,
        tiled=True,
    ).astype(jnp.float32)
    grad_full = lax.all_gather(cotangent, "tensor", axis=0, tiled=True)
    grad_down = dot_first(hidden_low, grad_full)
    grad_hidden = dot_last(grad_full, w_down)
    grad_gate_low = (grad_hidden * up_pre * sig_gate * (1.0 + gate_pre * (1.0 - sig_gate))).astype(
        jnp.bfloat16
    )
    grad_up_low = (grad_hidden * activated).astype(jnp.bfloat16)
    grad_wgate = dot_first(normed_two, grad_gate_low)
    grad_wup = dot_first(normed_two, grad_up_low)
    back_rows = lax.psum_scatter(
        dot_last(grad_gate_low, w_gate) + dot_last(grad_up_low, w_up),
        "tensor",
        scatter_dimension=0,
        tiled=True,
    )
    grad_resid = cotangent.astype(jnp.float32) + norm_back(back_rows, unit_two, scale_two, gain_mlp)
    grad_gain_two = jnp.sum(back_rows * unit_two, axis=0)
    grad_mixed = lax.all_gather(grad_resid.astype(jnp.bfloat16), "tensor", axis=0, tiled=True)
    grad_wout = dot_first(mixed_low, grad_mixed)
    grad_conv_out = dot_last(grad_mixed, w_out)
    grad_c = grad_conv_out * convolved
    seq_grad = (grad_conv_out * c_part).reshape(-1, LEN, channels)
    grad_gated = (
        taps[0] * shift_up(seq_grad, 2) + taps[1] * shift_up(seq_grad, 1) + taps[2] * seq_grad
    ).reshape(-1, channels)
    grad_taps = jnp.stack(
        [
            jnp.sum(seq_grad * back_two, axis=(0, 1)),
            jnp.sum(seq_grad * back_one, axis=(0, 1)),
            jnp.sum(seq_grad * seq_gated, axis=(0, 1)),
        ]
    )
    grad_proj_low = jnp.concatenate(
        [grad_gated * x_part, grad_c, grad_gated * b_part], axis=1
    ).astype(jnp.bfloat16)
    grad_win = dot_first(normed_one, grad_proj_low).reshape(model_width, 3, channels)
    back_first = lax.psum_scatter(
        dot_last(grad_proj_low, in_flat), "tensor", scatter_dimension=0, tiled=True
    )
    grad_gain_one = jnp.sum(back_first * unit_one, axis=0)
    grad_tokens = grad_resid + norm_back(back_first, unit_one, scale_one, gain_mix)
    grad_win, grad_taps, grad_wout, grad_wgate, grad_wup, grad_down = lax.psum(
        (grad_win, grad_taps, grad_wout, grad_wgate, grad_wup, grad_down), "dp"
    )
    grad_gain_one, grad_gain_two = lax.psum((grad_gain_one, grad_gain_two), ("dp", "tensor"))
    return (
        result,
        grad_tokens,
        grad_win,
        grad_taps,
        grad_wout,
        grad_wgate,
        grad_wup,
        grad_down,
        grad_gain_one,
        grad_gain_two,
    )


def solution(mesh):
    placed = (
        P(("dp", "tensor"), None),
        P(None, None, "tensor"),
        P(None, "tensor"),
        P("tensor", None),
        P(None, "tensor"),
        P(None, "tensor"),
        P("tensor", None),
        P(),
        P(),
        P(("dp", "tensor"), None),
    )
    return jax.shard_map(
        shards,
        mesh=mesh,
        in_specs=placed,
        out_specs=(
            P(("dp", "tensor"), None),
            P(("dp", "tensor"), None),
            P(None, None, "tensor"),
            P(None, "tensor"),
            P("tensor", None),
            P(None, "tensor"),
            P(None, "tensor"),
            P("tensor", None),
            P(),
            P(),
        ),
        check_vma=False,
    )
```

profile of v0, /device:TPU:0, one launch (start us, length us, event | category | flops | bytes accessed | tf_op | source)
XLA Modules:
  0.0 1082.2 jit_solution(13274525037778974450)
XLA Ops:
  7.2 1.7 fusion.15
  8.9 2.5 fusion.9
  11.5 2.6 copy.21
  14.1 34.7 %all-gather.5.cloned.1.call-done = bf16[2048,1024]{1,0:T(8,128)(2,1)} async-done(((bf16[512,1024]{1,0:T(8,128)(2,1)}), bf16[2048,1024]{1,0:T(8,128)(2,1)}) %all-gather.5.cloned.1.call-update) | async-done | bytes 4194320 | tf_op jit(solution)/shard_map/all_gather | solution.py:49
  48.8 5.7 fusion.26
  55.4 1.7 copy-done.1
  57.9 0.6 copy-done.6
  58.6 4.5 fusion.27
  63.2 71.8 %reduce-scatter.5.cloned.1.call-done = f32[512,1024]{1,0:T(8,128)} async-done(((f32[2048,1024]{1,0:T(8,128)}), f32[512,1024]{1,0:T(8,128)}) %reduce-scatter.5.cloned.1.call-update) | async-done | bytes 2097168 | tf_op jit(solution)/shard_map/reduce_scatter | solution.py:63
  135.0 1.9 multiply_reduce_fusion.5
  137.0 1.3 copy-done.2
  138.3 1.2 multiply_convert_fusion.3
  140.3 33.8 %all-gather.7.cloned.1.call-done = bf16[2048,1024]{1,0:T(8,128)(2,1)} async-done(((bf16[512,1024]{1,0:T(8,128)(2,1)}), bf16[2048,1024]{1,0:T(8,128)(2,1)}) %all-gather.7.cloned.1.call-update) | async-done | bytes 4194320 | tf_op jit(solution)/shard_map/all_gather | solution.py:70
  174.1 10.5 fusion.29
  184.7 8.0 fusion.28
  192.6 17.5 %all-gather.9.cloned.1.call-done = bf16[2048,1024]{1,0:T(8,128)(2,1)} async-done(((bf16[512,1024]{1,0:T(8,128)(2,1)}), bf16[2048,1024]{1,0:T(8,128)(2,1)}) %all-gather.9.cloned.1.call-update) | async-done | bytes 4194320 | tf_op jit(solution)/shard_map/all_gather | solution.py:84
  210.2 18.7 %multiply_convert_fusion = (bf16[2048,1152]{1,0:T(8,128)(2,1)}, bf16[2048,1152]{1,0:T(8,128)(2,1)}, bf16[2048,1152]{1,0:T(8,128)(2,1)}) fusion(f32[2048,1152]{1,0:T(8,128)} %fusion.28, f32[2048,1152]{1,0:T(8,128)} %fusion.29, bf16[2048,1024]{1,0:T(8,128)(2,1)} %all-gather.9.cloned.1.call-done, bf16[1152,1024]{1,0:T(8,128)(2,1)S(1)} %copy-done), kind=kOutput, calls=%fused_computation | convolution fusion | flops 4867227648 | bytes 39583744 | tf_op jit(solution)/shard_map/dot_general | solution.py:37
  228.9 7.7 fusion.30
  236.6 8.4 convolution_add_fusion
  245.2 71.6 %reduce-scatter.9.cloned.1.call-done = f32[512,1024]{1,0:T(8,128)} async-done(((f32[2048,1024]{1,0:T(8,128)}), f32[512,1024]{1,0:T(8,128)}) %reduce-scatter.9.cloned.1.call-update) | async-done | bytes 2097168 | tf_op jit(solution)/shard_map/reduce_scatter | solution.py:93
  316.8 3.0 multiply_reduce_fusion
  320.3 2.8 fusion.24
  323.2 34.6 %all-gather.11.cloned.1.call-done = bf16[2048,1024]{1,0:T(8,128)(2,1)} async-done(((bf16[512,1024]{1,0:T(8,128)(2,1)}), bf16[2048,1024]{1,0:T(8,128)(2,1)}) %all-gather.11.cloned.1.call-update) | async-done | bytes 4194320 | tf_op jit(solution)/shard_map/all_gather | solution.py:101
  357.8 6.0 multiply_reduce_fusion.3
  364.1 1.0 copy-done.4
  365.1 0.6 fusion.7
  365.7 3.1 fusion.16
  368.9 0.9 copy-done.18
  370.1 5.6 fusion.21
  375.8 9.6 convolution_convert_fusion
  385.8 11.5 %fusion.34 = f32[1152,1024]{1,0:T(8,128)} fusion(bf16[2048,1152]{1,0:T(8,128)(2,1)} %get-tuple-element.28, bf16[2048,1024]{1,0:T(8,128)(2,1)} %all-gather.9.cloned.1.call-done), kind=kOutput, calls=%fused_computation.69 | convolution fusion | flops 4831838208 | bytes 13631488 | tf_op jit(solution)/shard_map/dot_general | solution.py:31
  397.2 10.0 fusion.33
  407.3 10.2 fusion.32
  417.5 5.3 fusion.20
  422.8 3.8 copy.22
  426.6 4.8 fusion.31
  431.4 3.2 multiply_reduce_fusion.1
  434.6 21.8 %psum.57 = f32[3,256]{1,0:T(4,128)} all-reduce(f32[3,256]{1,0:T(4,128)S(1)} %pad_maximum_fusion.3), channel_id=1, replica_groups=mesh['dp'=8,'tensor'=4] {'dp'}, use_global_device_ids=true, to_apply=%region_12.13 | all-reduce | flops 768 | bytes 6144 | tf_op jit(solution)/shard_map/psum | solution.py:125
  456.4 2.3 fusion.14
  458.7 37.1 %all-reduce.4 = (f32[1024]{0:T(1024)}, f32[1024]{0:T(1024)}) all-reduce(f32[1024]{0:T(1024)S(1)} %get-tuple-element.14, f32[1024]{0:T(1024)S(1)} %get-tuple-element.10), channel_id=1, replica_groups=mesh['dp'=8,'tensor'=4] {'dp','tensor'}, use_global_device_ids=true, to_apply=%region_18.19 | all-reduce | flops 2048 | bytes 16384 | tf_op jit(solution)/shard_map/psum | solution.py:128
  495.9 5.3 fusion.13
  501.2 560.3 %all-reduce.8.cloned.1.call-done = (f32[1024,3,256]{2,0,1:T(8,128)}, f32[256,1024]{1,0:T(8,128)}, f32[1024,1152]{1,0:T(8,128)}, f32[1024,1152]{1,0:T(8,128)}, f32[1152,1024]{1,0:T(8,128)}) async-done(((f32[1024,3,256]{2,0,1:T(8,128)}, f32[256,1024]{1,0:T(8,128)}, f32[1024,1152]{1,0:T(8,128)}, f32[1024,1152]{1,0:T(8,128)}, f32[1152,1024]{1,0:T(8,128)}), (f32[1024,3,256]{2,0,1:T(8,128)}, ...) | async-done | bytes 18350096 | tf_op jit(solution)/shard_map/psum | solution.py:125
  1061.5 3.9 copy.28
  1065.4 1.0 copy.29
  1066.4 2.4 copy.30
  1068.8 1.6 copy-done.11
  1070.4 2.2 copy.31
  1073.0 2.2 copy.32
  (97 shorter events, 5.0 us)
Async XLA Ops:
  7.2 203.0 %copy-start = (bf16[1152,1024]{1,0:T(8,128)(2,1)S(1)}, bf16[1152,1024]{1,0:T(8,128)(2,1)}, u32[]{:S(2)}) copy-start(bf16[1152,1024]{1,0:T(8,128)(2,1)} %param.16) | copy-start | bytes 7077892
  7.2 41.6 %all-gather.5.cloned.1.call-start = ((), (), s32[]{:S(2)}) async-start(), calls=%async_computation.4 | async-start | bytes 5242880 | tf_op jit(solution)/shard_map/all_gather | solution.py:49
  8.9 5.2 copy-start.24
  11.4 2.7 copy-start.26
  11.4 123.5 %reduce-scatter.5.cloned.1.call-start = ((), (), s32[]{:S(2)}) async-start(), calls=%async_computation.5 | async-start | bytes 10485760 | tf_op jit(solution)/shard_map/reduce_scatter | solution.py:63
  54.5 2.7 copy-start.1
  54.8 3.1 copy-start.9
  57.2 1.4 copy-start.6
  57.2 1.4 copy-start.13
  58.6 4.5 copy-start.10
  63.1 71.9 %copy-start.5 = (bf16[512,1024]{1,0:T(8,128)(2,1)S(1)}, bf16[512,1024]{1,0:T(8,128)(2,1)}, u32[]{:S(2)}) copy-start(bf16[512,1024]{1,0:T(8,128)(2,1)} %param.10) | copy-start | bytes 3145732
  63.1 75.1 %copy-start.22 = (f32[1024]{0:T(1024)S(1)}, f32[1024]{0:T(1024)}, u32[]{:S(2)}) copy-start(f32[1024]{0:T(1024)} %param.18) | copy-start | bytes 12292
  63.2 111.0 %all-gather.7.cloned.1.call-start = ((), (), s32[]{:S(2)}) async-start(), calls=%async_computation.6 | async-start | bytes 5242880 | tf_op jit(solution)/shard_map/all_gather | solution.py:70
  136.9 1.3 copy-start.2
  139.5 70.6 %all-gather.9.cloned.1.call-start = ((), (), s32[]{:S(2)}) async-start(), calls=%async_computation.8 | async-start | bytes 5242880 | tf_op jit(solution)/shard_map/all_gather | solution.py:84
  140.1 176.8 %reduce-scatter.9.cloned.1.call-start = ((), (), s32[]{:S(2)}) async-start(), calls=%async_computation.9 | async-start | bytes 10485760 | tf_op jit(solution)/shard_map/reduce_scatter | solution.py:93
  174.1 10.6 copy-start.28
  174.1 10.6 copy-start.30
  210.1 18.7 %copy-start.31 = (bf16[1024,1152]{1,0:T(8,128)(2,1)S(1)}, bf16[1024,1152]{1,0:T(8,128)(2,1)}, u32[]{:S(2)}) copy-start(bf16[1024,1152]{1,0:T(8,128)(2,1)} %param.14) | copy-start | bytes 7077892
  228.9 7.7 copy-start.32
  228.9 7.7 copy-start.33
  245.0 112.8 %all-gather.11.cloned.1.call-start = ((), (), s32[]{:S(2)}) async-start(), calls=%async_computation.10 | async-start | bytes 5242880 | tf_op jit(solution)/shard_map/all_gather | solution.py:101
  316.8 3.0 copy-start.3
  316.8 3.5 copy-start.8
  323.2 133.3 %reduce-scatter.11.cloned.1.call-start = ((), (), s32[]{:S(2)}) async-start(), calls=%async_computation.11 | async-start | bytes 10485760 | tf_op jit(solution)/shard_map/reduce_scatter | solution.py:120
  357.8 6.0 copy-start.7
  363.8 1.3 copy-start.4
  364.1 4.7 copy-start.15
  365.7 4.4 copy-start.14
  368.8 1.0 copy-start.18
  368.8 1.3 copy-start.20
  375.8 120.1 %reduce-scatter.7.cloned.1.call-start = ((), (), s32[]{:S(2)}) async-start(), calls=%async_computation.7 | async-start | bytes 5242880 | tf_op jit(solution)/shard_map/reduce_scatter | solution.py:78
  385.5 676.0 %all-reduce.8.cloned.1.call-start = ((), (), s32[]{:S(2)}) async-start(), calls=%async_computation.12 | async-start | bytes 36700160 | tf_op jit(solution)/shard_map/psum | solution.py:125
  385.8 11.5 %copy-start.29 = (bf16[2048,1024]{1,0:T(8,128)(2,1)S(1)}, bf16[2048,1024]{1,0:T(8,128)(2,1)}, u32[]{:S(2)}) copy-start(bf16[2048,1024]{1,0:T(8,128)(2,1)} %all-gather.7.cloned.1.call-done) | copy-start | bytes 12582916
  407.3 10.2 copy-start.16
  407.3 10.2 copy-start.19
  407.3 10.2 copy-start.21
  407.3 10.2 copy-start.27
  431.4 25.1 %copy-start.23 = (f32[1024]{0:T(1024)S(1)}, f32[1024]{0:T(1024)}, u32[]{:S(2)}) copy-start(f32[1024]{0:T(1024)} %param.17) | copy-start | bytes 12292
  431.4 25.1 %copy-start.25 = (f32[512]{0:T(512)S(1)}, f32[512]{0:T(512)}, u32[]{:S(2)}) copy-start(f32[512]{0:T(512)} %copy-done.24) | copy-start | bytes 6148
  1061.5 3.9 copy-start.17
  1061.5 4.9 copy-start.12
  1066.4 4.0 copy-start.11
  1066.4 6.2 slice-start
  1070.4 2.6 slice-start.1
Sparse Core Ops, SparseCore 0:
  11.6 37.1 all-gather.4
  63.3 71.6 reduce-scatter.4
  139.6 34.4 all-gather.6
  175.6 34.4 all-gather.8
  245.1 71.6 reduce-scatter.8
  323.3 34.4 all-gather.10
  375.9 71.7 reduce-scatter.10
  450.4 44.9 reduce-scatter.6
  501.2 560.2 all-reduce.7
where the time goes:
time: 1090 us; the launch traced here: 1080 us
  waiting for transfers between devices  825 us (76%)
  matrix products  126 us (12%)
  blocking collectives  58.9 us (5%)
  other arithmetic  29.2 us (3%)
  local copies, waits for them, and re-layouts  27.1 us (2%)
  between operations  14.6 us (1%)
    psum x1, waiting for transfers between devices, shards(): lax.psum((grad_win, grad_taps, grad_wout, grad_wgate, grad_wup, grad_down...  560 us
    reduce_scatter x1, waiting for transfers between devices, shards(): lax.psum_scatter(jnp.dot(mixed_low, w_out, preferred_element_type=jnp.flo...  71.8 us
    reduce_scatter x1, waiting for transfers between devices, shards(): lax.psum_scatter(dot_last(grad_gate_low, w_gate) + dot_last(grad_up_low,...  71.6 us
    dot_general x5, matrix products, dot_last(): lax.dot_general(left, right, (((1,), (1,)), ((), ())), preferred_element_...  46.3 us
    dot_general x5, matrix products, dot_first(): lax.dot_general(left, right, (((0,), (0,)), ((), ())), preferred_element_...  41.7 us
    psum x1, blocking collectives, shards(): lax.psum((grad_gain_one, grad_gain_two), ('dp', 'tensor'))  37.1 us
    all_gather x1, waiting for transfers between devices, shards(): lax.all_gather((unit_one * gain_mix).astype(jnp.bfloat16), 'tensor', axis...  34.7 us
    all_gather x1, waiting for transfers between devices, shards(): lax.all_gather(grad_resid.astype(jnp.bfloat16), 'tensor', axis=0, tiled=T...  34.6 us
  transfers between devices with their start and end apart: 9, of which 7 were waited for; matrix products, arithmetic and copies ran while one was open for 8% of the time, Pallas kernels for 0%

commit v1 on v0

--- a/solution.py
+++ b/solution.py
@@ -140,6 +140,199 @@
     )
 
 
+def swap(values, axis, step):
+    count = lax.axis_size(axis)
+    return lax.ppermute(values, axis, [(i, i ^ step) for i in range(count)])
+
+
+def part(values, index):
+    size = values.shape[0] // 2
+    return lax.dynamic_slice_in_dim(values, index * size, size, axis=0)
+
+
+def in_order(bit, mine, other):
+    return jnp.concatenate(
+        [jnp.where(bit == 0, mine, other), jnp.where(bit == 0, other, mine)], axis=0
+    )
+
+
+def halving(values, order):
+    place = lax.axis_index("dp")
+    piece = values.astype(jnp.bfloat16)
+    for step in order:
+        bit = (place // step) % 2
+        arrived = swap(part(piece, 1 - bit), "dp", step)
+        piece = (
+            part(piece, bit).astype(jnp.float32) + arrived.astype(jnp.float32)
+        ).astype(jnp.bfloat16)
+    for step in reversed(order):
+        bit = (place // step) % 2
+        piece = in_order(bit, piece, swap(piece, "dp", step))
+    return piece
+
+
+def dp_sum(values):
+    rows = values.shape[0]
+    cut = max(rows * 5 // 8 // 128, 1) * 128
+    return jnp.concatenate(
+        [halving(values[:cut], (1, 2, 4)), halving(values[cut:], (2, 1, 4))], axis=0
+    ).astype(jnp.float32)
+
+
+def small_sum(values, axis):
+    step = 1
+    while step < lax.axis_size(axis):
+        values = values + swap(values, axis, step)
+        step *= 2
+    return values
+
+
+def gather_pair(own, core, after=None):
+    near = in_order(core, own, swap(own, "tensor", 1))
+    if after is not None:
+        own, _ = lax.optimization_barrier((own, after))
+    across = swap(own, "tensor", 2)
+    far = in_order(core, across, swap(across, "tensor", 1))
+    return near, far, across
+
+
+def reduce_far(far, core):
+    low = jnp.bfloat16
+    arrived = swap(part(far, 1 - core), "tensor", 1)
+    total = (part(far, core).astype(jnp.float32) + arrived.astype(jnp.float32)).astype(low)
+    return swap(total, "tensor", 2)
+
+
+def reduce_near(near, core, crossed):
+    arrived = swap(part(near, 1 - core), "tensor", 1)
+    return (
+        part(near, core).astype(jnp.float32)
+        + arrived.astype(jnp.float32)
+        + crossed.astype(jnp.float32)
+    )
+
+
+def dot(left, right):
+    return jnp.dot(left, right, preferred_element_type=jnp.float32)
+
+
+def down(values, shift_by):
+    return jnp.pad(values, ((shift_by, 0), (0, 0)))[: values.shape[0]]
+
+
+def up(values, shift_by):
+    return jnp.pad(values, ((0, shift_by), (0, 0)))[shift_by:]
+
+
+def conv_forward(normed, in_flat, taps):
+    channels = taps.shape[1]
+    projected = dot(normed, in_flat)
+    b_part = projected[:, :channels]
+    c_part = projected[:, channels : 2 * channels]
+    x_part = projected[:, 2 * channels :]
+    gated = b_part * x_part
+    convolved = taps[0] * down(gated, 2) + taps[1] * down(gated, 1) + taps[2] * gated
+    mixed = (c_part * convolved).astype(jnp.bfloat16)
+    return mixed, (b_part, c_part, x_part, gated, convolved)
+
+
+def conv_backward(grad_mixed, kept, w_out, taps):
+    b_part, c_part, x_part, gated, convolved = kept
+    grad_conv_out = dot_last(grad_mixed, w_out)
+    grad_c = grad_conv_out * convolved
+    grad_conv = grad_conv_out * c_part
+    grad_gated = taps[0] * up(grad_conv, 2) + taps[1] * up(grad_conv, 1) + taps[2] * grad_conv
+    grad_taps = jnp.stack(
+        [
+            jnp.sum(grad_conv * down(gated, 2), axis=0),
+            jnp.sum(grad_conv * down(gated, 1), axis=0),
+            jnp.sum(grad_conv * gated, axis=0),
+        ]
+    )
+    grad_projected = jnp.concatenate(
+        [grad_gated * x_part, grad_c, grad_gated * b_part], axis=1
+    ).astype(jnp.bfloat16)
+    return grad_projected, grad_taps
+
+
+def mlp_forward(normed, w_gate, w_up):
+    gate_pre = dot(normed, w_gate)
+    up_pre = dot(normed, w_up)
+    sig_gate = jax.nn.sigmoid(gate_pre)
+    hidden = (gate_pre * sig_gate * up_pre).astype(jnp.bfloat16)
+    return hidden, (gate_pre, up_pre, sig_gate)
+
+
+def mlp_backward(grad_out, kept, w_gate, w_up, w_down):
+    gate_pre, up_pre, sig_gate = kept
+    grad_hidden = dot_last(grad_out, w_down)
+    grad_gate = (grad_hidden * up_pre * sig_gate * (1.0 + gate_pre * (1.0 - sig_gate))).astype(
+        jnp.bfloat16
+    )
+    grad_up = (grad_hidden * gate_pre * sig_gate).astype(jnp.bfloat16)
+    back = (dot_last(grad_gate, w_gate) + dot_last(grad_up, w_up)).astype(jnp.bfloat16)
+    return grad_gate, grad_up, back
+
+
+def pair_shards(
+    tokens, w_in, conv_kernel, w_out, w_gate, w_up, w_down, gain_mix, gain_mlp, cotangent
+):
+    low = jnp.bfloat16
+    model_width = tokens.shape[1]
+    channels = conv_kernel.shape[1]
+    core = lax.axis_index("tensor") % 2
+    in_flat = w_in.reshape(model_width, 3 * channels)
+    taps = conv_kernel.astype(jnp.float32)
+    inputs = tokens.astype(jnp.float32)
+    unit_one, scale_one = rms_scale(inputs)
+    one_near, one_far, _ = gather_pair((unit_one * gain_mix).astype(low), core)
+    mixed_near, kept_near = conv_forward(one_near, in_flat, taps)
+    mixed_far, kept_far = conv_forward(one_far, in_flat, taps)
+    crossed = reduce_far(dot(mixed_far, w_out).astype(low), core)
+    resid = inputs + reduce_near(dot(mixed_near, w_out).astype(low), core, crossed)
+    unit_two, scale_two = rms_scale(resid)
+    two_near, two_far, two_across = gather_pair((unit_two * gain_mlp).astype(low), core)
+    cot_near, cot_far, _ = gather_pair(cotangent, core, after=two_across)
+    hidden_near, mlp_near = mlp_forward(two_near, w_gate, w_up)
+    gate_near, up_near, back_near = mlp_backward(cot_near, mlp_near, w_gate, w_up, w_down)
+    hidden_far, mlp_far = mlp_forward(two_far, w_gate, w_up)
+    out_crossed = reduce_far(dot(hidden_far, w_down).astype(low), core)
+    gate_far, up_far, back_far = mlp_backward(cot_far, mlp_far, w_gate, w_up, w_down)
+    back_crossed = reduce_far(back_far, core)
+    grad_down = dp_sum(dot_first(hidden_near, cot_near) + dot_first(hidden_far, cot_far))
+    grad_wgate = dp_sum(dot_first(two_near, gate_near) + dot_first(two_far, gate_far))
+    grad_wup = dp_sum(dot_first(two_near, up_near) + dot_first(two_far, up_far))
+    result = resid + reduce_near(dot(hidden_near, w_down).astype(low), core, out_crossed)
+    back_rows = reduce_near(back_near, core, back_crossed)
+    grad_resid = cotangent.astype(jnp.float32) + norm_back(back_rows, unit_two, scale_two, gain_mlp)
+    gain_two = jnp.sum(back_rows * unit_two, axis=0)
+    gm_near, gm_far, _ = gather_pair(grad_resid.astype(low), core)
+    gp_near, taps_near = conv_backward(gm_near, kept_near, w_out, taps)
+    gp_far, taps_far = conv_backward(gm_far, kept_far, w_out, taps)
+    first_crossed = reduce_far(dot_last(gp_far, in_flat).astype(low), core)
+    grad_wout = dp_sum(dot_first(mixed_near, gm_near) + dot_first(mixed_far, gm_far))
+    grad_win = dp_sum(dot_first(one_near, gp_near) + dot_first(one_far, gp_far))
+    back_first = reduce_near(dot_last(gp_near, in_flat).astype(low), core, first_crossed)
+    gain_one = jnp.sum(back_first * unit_one, axis=0)
+    grad_tokens = grad_resid + norm_back(back_first, unit_one, scale_one, gain_mix)
+    gains = small_sum(jnp.stack([gain_one, gain_two]), "tensor")
+    small = small_sum(
+        jnp.concatenate([gains.reshape(-1), (taps_near + taps_far).reshape(-1)]), "dp"
+    )
+    return (
+        result,
+        grad_tokens,
+        grad_win.reshape(model_width, 3, channels),
+        small[2 * model_width :].reshape(3, channels),
+        grad_wout,
+        grad_wgate,
+        grad_wup,
+        grad_down,
+        small[:model_width],
+        small[model_width : 2 * model_width],
+    )
+
+
 def solution(mesh):
     placed = (
         P(("dp", "tensor"), None),
@@ -153,8 +346,9 @@
         P(),
         P(("dp", "tensor"), None),
     )
+    paired = mesh.shape["tensor"] == 4 and mesh.shape["dp"] == 8
     return jax.shard_map(
-        shards,
+        pair_shards if paired else shards,
         mesh=mesh,
         in_specs=placed,
         out_specs=(

time: 1090 us -> 617 us (0.57)
  waiting for transfers between devices: 825 us -> 321 us
  starting transfers between devices: 1.01 us -> 85.4 us
  blocking collectives: 58.9 us -> 0 us
  other arithmetic: 29.2 us -> 52.5 us
  between operations: 14.6 us -> 3.32 us
    psum x1 -> x0, waiting for transfers between devices: 560 us -> none  [shards(): lax.psum((grad_win, grad_taps, grad_wout, grad_wgate, grad_wup, grad_down...]
    ppermute x0 -> x89, waiting for transfers between devices: none -> 321 us  [swap(): return lax.ppermute(values, axis, [(i, i ^ step) for i in range(count)])]
    reduce_scatter x4 -> x0, waiting for transfers between devices: 143 us -> none  [the longest x1 71.8 us: shards(): lax.psum_scatter(jnp.dot(mixed_low, w_out, preferred_element_type=jnp.flo...]
    all_gather x4 -> x0, waiting for transfers between devices: 121 us -> none  [the longest x1 34.7 us: shards(): lax.all_gather((unit_one * gain_mix).astype(jnp.bfloat16), 'tensor', axis...]
    ppermute x0 -> x89, starting transfers between devices: none -> 85.4 us  [swap(): return lax.ppermute(values, axis, [(i, i ^ step) for i in range(count)])]
    psum x2 -> x0, blocking collectives: 58.9 us -> none  [the longest x1 37.1 us: shards(): lax.psum((grad_gain_one, grad_gain_two), ('dp', 'tensor'))]
    convert_element_type x4 -> x43, other arithmetic: 6.85 us -> 27.5 us  [the longest x5 12.2 us: dp_sum(): return jnp.concatenate([halving(values[:cut], (1, 2, 4)), halving(values[...]
    select_n x0 -> x38, other arithmetic: none -> 13 us  [in_order(): jnp.where(bit == 0, mine, other)]
  transfers between devices with their start and end apart: 9 -> 89, of which waited for: 7 -> 48; matrix products, arithmetic and copies ran while one was open for 8% -> 26% of each run, Pallas kernels for 0% -> 0%
where the time goes in v1:
time: 617 us; the launch traced here: 613 us
  waiting for transfers between devices  321 us (52%)
  matrix products  121 us (20%)
  starting transfers between devices  85.4 us (14%)
  other arithmetic  52.5 us (9%)
  local copies, waits for them, and re-layouts  29.3 us (5%)
    ppermute x89, waiting for transfers between devices, swap(): return lax.ppermute(values, axis, [(i, i ^ step) for i in range(count)])  321 us
    ppermute x89, starting transfers between devices, swap(): return lax.ppermute(values, axis, [(i, i ^ step) for i in range(count)])  85.4 us
    dot_general x10, matrix products, dot(): return jnp.dot(left, right, preferred_element_type=jnp.float32)  45.5 us
    dot_general x10, matrix products, dot_last(): lax.dot_general(left, right, (((1,), (1,)), ((), ())), preferred_element_...  41.1 us
    dot_general x10, matrix products, dot_first(): lax.dot_general(left, right, (((0,), (0,)), ((), ())), preferred_element_...  34.9 us
    unnamed x133, local copies, waits for them, and re-layouts  19.9 us
    select_n x38, other arithmetic, in_order(): jnp.where(bit == 0, mine, other)  13 us
  transfers between devices with their start and end apart: 89, of which 48 were waited for; matrix products, arithmetic and copies ran while one was open for 26% of the time, Pallas kernels for 0%

profile of v1, /device:TPU:0, one launch (start us, length us, event | category | flops | bytes accessed | tf_op | source)
XLA Modules:
  0.0 613.1 jit_solution(16987118469629806970)
XLA Ops:
  7.9 23.5 %collective-permute-done.2 = bf16[512,1024]{1,0:T(8,128)(2,1)} collective-permute-done((bf16[512,1024]{1,0:T(8,128)(2,1)}, bf16[512,1024]{1,0:T(8,128)(2,1)}, u32[]{:S(2)}, u32[]{:S(2)}) %collective-permute-start.2) | collective-permute-done | bytes 1048608 | tf_op jit(solution)/shard_map/ppermute | solution.py:145
  55.9 23.6 %collective-permute-done.5 = bf16[512,1024]{1,0:T(8,128)(2,1)S(1)} collective-permute-done((bf16[512,1024]{1,0:T(8,128)(2,1)S(1)}, bf16[512,1024]{1,0:T(8,128)(2,1)S(1)}, u32[]{:S(2)}, u32[]{:S(2)}) %collective-permute-start.5) | collective-permute-done | bytes 1048608 | tf_op jit(solution)/shard_map/ppermute | solution.py:145
  87.6 5.3 fusion.48
  92.9 5.5 fusion.49
  98.4 8.9 %multiply_convert_fusion.2 = (bf16[1024,1152]{1,0:T(8,128)(2,1)}, bf16[1024,1152]{1,0:T(8,128)(2,1)S(1)}, bf16[1024,1152]{1,0:T(8,128)(2,1)S(1)}) fusion(f32[1024,1152]{1,0:T(8,128)} %fusion.49, f32[1024,1152]{1,0:T(8,128)} %fusion.48, bf16[1152,1024]{1,0:T(8,128)(2,1)S(1)} %copy-done, bf16[512,1024]{1,0:T(8,128)(2,1)S(1)} %get-tuple-element.58, ...), kind=kOutput, calls=%fused_computation.5 | convolution fusion | flops 2438987776 | bytes 20971520 | tf_op jit(solution)/shard_map/dot_general | solution.py:37
  108.7 4.3 fusion.15
  113.0 4.7 convolution_convert_fusion.1
  125.4 4.6 fusion.46
  130.0 4.6 fusion.47
  134.6 8.5 %collective-permute-done.14 = bf16[512,1024]{1,0:T(8,128)(2,1)S(1)} collective-permute-done((bf16[512,1024]{1,0:T(8,128)(2,1)}, bf16[512,1024]{1,0:T(8,128)(2,1)S(1)}, u32[]{:S(2)}, u32[]{:S(2)}) %collective-permute-start.14) | collective-permute-done | bytes 1048608 | tf_op jit(solution)/shard_map/ppermute | solution.py:145
  143.2 15.1 %fusion.44 = f32[1024,1152]{1,0:T(8,128)} fusion(bf16[1024,1152]{1,0:T(8,128)(2,1)S(1)} %copy-done.55, bf16[512,1024]{1,0:T(8,128)(2,1)S(1)} %get-tuple-element.64, bf16[512,1024]{1,0:T(8,128)(2,1)S(1)} %get-tuple-element.63), kind=kOutput, calls=%fused_computation.296 | convolution fusion | flops 2420113408 | bytes 9175040 | tf_op jit(solution)/shard_map/dot_general | solution.py:216
  158.3 5.3 fusion.45
  163.7 9.6 %multiply_convert_fusion = (bf16[1024,1152]{1,0:T(8,128)(2,1)}, bf16[1024,1152]{1,0:T(8,128)(2,1)}, bf16[1024,1152]{1,0:T(8,128)(2,1)}) fusion(f32[1024,1152]{1,0:T(8,128)} %fusion.45, f32[1024,1152]{1,0:T(8,128)} %fusion.44, bf16[1152,1024]{1,0:T(8,128)(2,1)S(1)} %copy-done, bf16[512,1024]{1,0:T(8,128)(2,1)S(1)} %get-tuple-element.60, ...), kind=kOutput, calls=%fused_computation.3 | convolution fusion | flops 2438987776 | bytes 20971520 | tf_op jit(solution)/shard_map/dot_general | solution.py:37
  173.4 5.3 add_convert_fusion
  178.9 5.7 add_convert_fusion.1
  184.8 4.9 add_convert_fusion.2
  194.5 4.5 fusion.57
  203.5 5.1 add_convert_fusion.3
  208.9 15.3 %collective-permute-done.71 = bf16[192,1152]{1,0:T(8,128)(2,1)S(1)} collective-permute-done((bf16[192,1152]{1,0:T(8,128)(2,1)S(1)}, bf16[192,1152]{1,0:T(8,128)(2,1)S(1)}, u32[]{:S(2)}, u32[]{:S(2)}) %collective-permute-start.71) | collective-permute-done | bytes 442400 | tf_op jit(solution)/shard_map/ppermute | solution.py:145
  226.0 9.8 %collective-permute-done.59 = bf16[192,1152]{1,0:T(8,128)(2,1)S(1)} collective-permute-done((bf16[192,1152]{1,0:T(8,128)(2,1)S(1)}, bf16[192,1152]{1,0:T(8,128)(2,1)S(1)}, u32[]{:S(2)}, u32[]{:S(2)}) %collective-permute-start.59) | collective-permute-done | bytes 442400 | tf_op jit(solution)/shard_map/ppermute | solution.py:145
  238.7 18.7 %collective-permute-done.72 = bf16[96,1152]{1,0:T(8,128)(2,1)S(1)} collective-permute-done((bf16[96,1152]{1,0:T(8,128)(2,1)S(1)}, bf16[96,1152]{1,0:T(8,128)(2,1)S(1)}, u32[]{:S(2)}, u32[]{:S(2)}) %collective-permute-start.72) | collective-permute-done | bytes 221216 | tf_op jit(solution)/shard_map/ppermute | solution.py:145
  258.0 5.3 collective-permute-done.60
  267.1 5.6 collective-permute-done.73
  273.1 7.6 %collective-permute-done.61 = bf16[48,1152]{1,0:T(8,128)(2,1)S(1)} collective-permute-done((bf16[48,1152]{1,0:T(8,128)(2,1)S(1)}, bf16[48,1152]{1,0:T(8,128)(2,1)S(1)}, u32[]{:S(2)}, u32[]{:S(2)}) %collective-permute-start.61) | collective-permute-done | bytes 110624 | tf_op jit(solution)/shard_map/ppermute | solution.py:145
  282.9 6.2 %collective-permute-done.74 = bf16[48,1152]{1,0:T(8,128)(2,1)S(1)} collective-permute-done((bf16[48,1152]{1,0:T(8,128)(2,1)S(1)}, bf16[48,1152]{1,0:T(8,128)(2,1)S(1)}, u32[]{:S(2)}, u32[]{:S(2)}) %collective-permute-start.74) | collective-permute-done | bytes 110624 | tf_op jit(solution)/shard_map/ppermute | solution.py:145
  307.3 15.9 %collective-permute-done.86 = bf16[64,1024]{1,0:T(8,128)(2,1)S(1)} collective-permute-done((bf16[64,1024]{1,0:T(8,128)(2,1)S(1)}, bf16[64,1024]{1,0:T(8,128)(2,1)S(1)}, u32[]{:S(2)}, u32[]{:S(2)}) %collective-permute-start.86) | collective-permute-done | bytes 131104 | tf_op jit(solution)/shard_map/ppermute | solution.py:145
  325.4 6.1 collective-permute-done.75
  341.3 9.5 %collective-permute-done.67 = bf16[80,1152]{1,0:T(8,128)(2,1)S(1)} collective-permute-done((bf16[80,1152]{1,0:T(8,128)(2,1)S(1)}, bf16[80,1152]{1,0:T(8,128)(2,1)S(1)}, u32[]{:S(2)}, u32[]{:S(2)}) %collective-permute-start.67) | collective-permute-done | bytes 184352 | tf_op jit(solution)/shard_map/ppermute | solution.py:145
  350.8 11.7 %collective-permute-done.55 = bf16[80,1152]{1,0:T(8,128)(2,1)S(1)} collective-permute-done((bf16[80,1152]{1,0:T(8,128)(2,1)S(1)}, bf16[80,1152]{1,0:T(8,128)(2,1)S(1)}, u32[]{:S(2)}, u32[]{:S(2)}) %collective-permute-start.55) | collective-permute-done | bytes 184352 | tf_op jit(solution)/shard_map/ppermute | solution.py:145
  362.6 10.6 %collective-permute-done.80 = bf16[80,1024]{1,0:T(8,128)(2,1)S(1)} collective-permute-done((bf16[80,1024]{1,0:T(8,128)(2,1)S(1)}, bf16[80,1024]{1,0:T(8,128)(2,1)S(1)}, u32[]{:S(2)}, u32[]{:S(2)}) %collective-permute-start.80) | collective-permute-done | bytes 163872 | tf_op jit(solution)/shard_map/ppermute | solution.py:145
  374.0 9.8 %collective-permute-done.68 = bf16[80,1152]{1,0:T(8,128)(2,1)S(1)} collective-permute-done((bf16[80,1152]{1,0:T(8,128)(2,1)S(1)}, bf16[80,1152]{1,0:T(8,128)(2,1)S(1)}, u32[]{:S(2)}, u32[]{:S(2)}) %collective-permute-start.68) | collective-permute-done | bytes 184352 | tf_op jit(solution)/shard_map/ppermute | solution.py:145
  387.3 5.1 collective-permute-done.56
  394.7 10.7 %collective-permute-done.64 = bf16[192,1152]{1,0:T(8,128)(2,1)S(1)} collective-permute-done((bf16[192,1152]{1,0:T(8,128)(2,1)S(1)}, bf16[192,1152]{1,0:T(8,128)(2,1)S(1)}, u32[]{:S(2)}, u32[]{:S(2)}) %collective-permute-start.64) | collective-permute-done | bytes 442400 | tf_op jit(solution)/shard_map/ppermute | solution.py:145
  407.3 5.2 collective-permute-done.81
  413.8 7.2 %collective-permute-done.88 = bf16[256,1024]{1,0:T(8,128)(2,1)S(1)} collective-permute-done((bf16[256,1024]{1,0:T(8,128)(2,1)S(1)}, bf16[256,1024]{1,0:T(8,128)(2,1)S(1)}, u32[]{:S(2)}, u32[]{:S(2)}) %collective-permute-start.88) | collective-permute-done | bytes 524320 | tf_op jit(solution)/shard_map/ppermute | solution.py:145
  421.2 5.7 collective-permute-done.69
  427.2 7.2 %collective-permute-done.57 = bf16[160,1152]{1,0:T(8,128)(2,1)S(1)} collective-permute-done((bf16[160,1152]{1,0:T(8,128)(2,1)S(1)}, bf16[160,1152]{1,0:T(8,128)(2,1)S(1)}, u32[]{:S(2)}, u32[]{:S(2)}) %collective-permute-start.57) | collective-permute-done | bytes 368672 | tf_op jit(solution)/shard_map/ppermute | solution.py:145
  439.3 4.6 fusion.52
  444.7 7.4 %collective-permute-done.82 = bf16[320,1024]{1,0:T(8,128)(2,1)S(1)} collective-permute-done((bf16[320,1024]{1,0:T(8,128)(2,1)S(1)}, bf16[320,1024]{1,0:T(8,128)(2,1)S(1)}, u32[]{:S(2)}, u32[]{:S(2)}) %collective-permute-start.82) | collective-permute-done | bytes 655392 | tf_op jit(solution)/shard_map/ppermute | solution.py:145
  455.2 10.3 %collective-permute-done.70 = bf16[320,1152]{1,0:T(8,128)(2,1)S(1)} collective-permute-done((bf16[320,1152]{1,0:T(8,128)(2,1)S(1)}, bf16[320,1152]{1,0:T(8,128)(2,1)S(1)}, u32[]{:S(2)}, u32[]{:S(2)}) %collective-permute-start.70) | collective-permute-done | bytes 737312 | tf_op jit(solution)/shard_map/ppermute | solution.py:145
  468.3 5.1 collective-permute-done.58
  508.0 6.9 %collective-permute-done.42 = bf16[32,1024]{1,0:T(8,128)(2,1)S(1)} collective-permute-done((bf16[32,1024]{1,0:T(8,128)(2,1)S(1)}, bf16[32,1024]{1,0:T(8,128)(2,1)S(1)}, u32[]{:S(2)}, u32[]{:S(2)}) %collective-permute-start.42) | collective-permute-done | bytes 65568 | tf_op jit(solution)/shard_map/ppermute | solution.py:145
  519.2 4.8 collective-permute-done.43
  524.0 4.9 collective-permute-done.49
  529.2 4.6 collective-permute-done.44
  534.1 4.4 collective-permute-done.50
  576.8 4.0 collective-permute-done.28
  606.9 4.8 fusion.8
  (472 shorter events, 225.7 us)
Async XLA Ops:
  5.0 26.4 %collective-permute-start.2 = (bf16[512,1024]{1,0:T(8,128)(2,1)}, bf16[512,1024]{1,0:T(8,128)(2,1)}, u32[]{:S(2)}, u32[]{:S(2)}) collective-permute-start(bf16[512,1024]{1,0:T(8,128)(2,1)} %fusion.4), channel_id=1, source_target_pairs={{0,2},{1,3},{2,0},{3,1},{4,6},{5,7},{6,4},{7,5},{8,10},{9,11},{10,... | collective-permute-start | bytes 3145736 | tf_op jit(solution)/shard_map/ppermute | solution.py:145
  7.9 26.1 %collective-permute-start = (bf16[512,1024]{1,0:T(8,128)(2,1)}, bf16[512,1024]{1,0:T(8,128)(2,1)}, u32[]{:S(2)}, u32[]{:S(2)}) collective-permute-start(bf16[512,1024]{1,0:T(8,128)(2,1)} %fusion.4), channel_id=1, source_target_pairs={{0,1},{1,0},{2,3},{3,2},{4,5},{5,4},{6,7},{7,6},{8,9},{9,8},{10,11... | collective-permute-start | bytes 3145736 | tf_op jit(solution)/shard_map/ppermute | solution.py:145
  54.0 25.5 %collective-permute-start.5 = (bf16[512,1024]{1,0:T(8,128)(2,1)S(1)}, bf16[512,1024]{1,0:T(8,128)(2,1)S(1)}, u32[]{:S(2)}, u32[]{:S(2)}) collective-permute-start(bf16[512,1024]{1,0:T(8,128)(2,1)S(1)} %add_convert_fusion.9), channel_id=1, source_target_pairs={{0,2},{1,3},{2,0},{3,1},{4,6},{5,7},{6,4},{7,5},{8,10},{9,11},{10,... | collective-permute-start | bytes 3145736 | tf_op jit(solution)/shard_map/ppermute | solution.py:145
  55.9 26.3 %collective-permute-start.12 = (bf16[512,1024]{1,0:T(8,128)(2,1)}, bf16[512,1024]{1,0:T(8,128)(2,1)}, u32[]{:S(2)}, u32[]{:S(2)}) collective-permute-start(bf16[512,1024]{1,0:T(8,128)(2,1)} %param.19), channel_id=1, source_target_pairs={{0,1},{1,0},{2,3},{3,2},{4,5},{5,4},{6,7},{7,6},{8,9},{9,8},{10,11... | collective-permute-start | bytes 3145736 | tf_op jit(solution)/shard_map/ppermute | solution.py:145
  84.0 33.8 %collective-permute-start.8 = (bf16[512,1024]{1,0:T(8,128)(2,1)S(1)}, bf16[512,1024]{1,0:T(8,128)(2,1)S(1)}, u32[]{:S(2)}, u32[]{:S(2)}) collective-permute-start(bf16[512,1024]{1,0:T(8,128)(2,1)S(1)} %multiply_convert_fusion.6), channel_id=1, source_target_pairs={{0,2},{1,3},{2,0},{3,1},{4,6},{5,7},{6,4},{7,5},{8,10},{9,11},{10,... | collective-permute-start | bytes 3145736 | tf_op jit(solution)/shard_map/ppermute | solution.py:145
  117.8 25.3 %collective-permute-start.14 = (bf16[512,1024]{1,0:T(8,128)(2,1)}, bf16[512,1024]{1,0:T(8,128)(2,1)S(1)}, u32[]{:S(2)}, u32[]{:S(2)}) collective-permute-start(bf16[512,1024]{1,0:T(8,128)(2,1)} %param.19), channel_id=1, source_target_pairs={{0,2},{1,3},{2,0},{3,1},{4,6},{5,7},{6,4},{7,5},{8,10},{9,11},{10,... | collective-permute-start | bytes 3145736 | tf_op jit(solution)/shard_map/ppermute | solution.py:145
  124.6 311.6 %collective-permute-start.13 = (bf16[512,1024]{1,0:T(8,128)(2,1)S(1)}, bf16[512,1024]{1,0:T(8,128)(2,1)S(1)}, u32[]{:S(2)}, u32[]{:S(2)}) collective-permute-start(bf16[512,1024]{1,0:T(8,128)(2,1)S(1)} %constant_dynamic-slice_fusion.33), channel_id=1, source_target_pairs={{0,1},{1,0},{2,3},{3,2},{4,5},{5,4},{6,7},{7,6},{8,9},{9,8},{10,11... | collective-permute-start | bytes 3145736 | tf_op jit(solution)/shard_map/ppermute | solution.py:145
  124.8 18.3 %collective-permute-start.9 = (bf16[512,1024]{1,0:T(8,128)(2,1)S(1)}, bf16[512,1024]{1,0:T(8,128)(2,1)S(1)}, u32[]{:S(2)}, u32[]{:S(2)}) collective-permute-start(bf16[512,1024]{1,0:T(8,128)(2,1)S(1)} %collective-permute-done.8), channel_id=1, source_target_pairs={{0,1},{1,0},{2,3},{3,2},{4,5},{5,4},{6,7},{7,6},{8,9},{9,8},{10,11... | collective-permute-start | bytes 3145736 | tf_op jit(solution)/shard_map/ppermute | solution.py:145
  143.1 20.5 %collective-permute-start.15 = (bf16[512,1024]{1,0:T(8,128)(2,1)S(1)}, bf16[512,1024]{1,0:T(8,128)(2,1)S(1)}, u32[]{:S(2)}, u32[]{:S(2)}) collective-permute-start(bf16[512,1024]{1,0:T(8,128)(2,1)S(1)} %collective-permute-done.14), channel_id=1, source_target_pairs={{0,1},{1,0},{2,3},{3,2},{4,5},{5,4},{6,7},{7,6},{8,9},{9,8},{10,11... | collective-permute-start | bytes 3145736 | tf_op jit(solution)/shard_map/ppermute | solution.py:145
  199.0 37.8 %collective-permute-start.77 = (bf16[320,1024]{1,0:T(8,128)(2,1)S(1)}, bf16[320,1024]{1,0:T(8,128)(2,1)S(1)}, u32[]{:S(2)}, u32[]{:S(2)}) collective-permute-start(bf16[320,1024]{1,0:T(8,128)(2,1)S(1)} %constant_dynamic-slice_fusion.5), channel_id=1, source_target_pairs={{0,4},{4,0},{8,12},{12,8},{16,20},{20,16},{24,28},{28,24},{1,5},{5... | collective-permute-start | bytes 1966088 | tf_op jit(solution)/shard_map/ppermute | solution.py:145
  200.7 35.8 %collective-permute-start.83 = (bf16[256,1024]{1,0:T(8,128)(2,1)S(1)}, bf16[256,1024]{1,0:T(8,128)(2,1)S(1)}, u32[]{:S(2)}, u32[]{:S(2)}) collective-permute-start(bf16[256,1024]{1,0:T(8,128)(2,1)S(1)} %constant_dynamic-slice_fusion.2), channel_id=1, source_target_pairs={{0,8},{4,12},{8,0},{12,4},{16,24},{20,28},{24,16},{28,20},{1,9},{5... | collective-permute-start | bytes 1572872 | tf_op jit(solution)/shard_map/ppermute | solution.py:145
  202.4 61.0 %collective-permute-start.65 = (bf16[320,1152]{1,0:T(8,128)(2,1)S(1)}, bf16[320,1152]{1,0:T(8,128)(2,1)S(1)}, u32[]{:S(2)}, u32[]{:S(2)}) collective-permute-start(bf16[320,1152]{1,0:T(8,128)(2,1)S(1)} %constant_dynamic-slice_fusion.11), channel_id=1, source_target_pairs={{0,4},{4,0},{8,12},{12,8},{16,20},{20,16},{24,28},{28,24},{1,5},{5... | collective-permute-start | bytes 2211848 | tf_op jit(solution)/shard_map/ppermute | solution.py:145
  203.0 21.3 %collective-permute-start.71 = (bf16[192,1152]{1,0:T(8,128)(2,1)S(1)}, bf16[192,1152]{1,0:T(8,128)(2,1)S(1)}, u32[]{:S(2)}, u32[]{:S(2)}) collective-permute-start(bf16[192,1152]{1,0:T(8,128)(2,1)S(1)} %constant_dynamic-slice_fusion.8), channel_id=1, source_target_pairs={{0,8},{4,12},{8,0},{12,4},{16,24},{20,28},{24,16},{28,20},{1,9},{5... | collective-permute-start | bytes 1327112 | tf_op jit(solution)/shard_map/ppermute | solution.py:145
  224.3 11.5 %collective-permute-start.59 = (bf16[192,1152]{1,0:T(8,128)(2,1)S(1)}, bf16[192,1152]{1,0:T(8,128)(2,1)S(1)}, u32[]{:S(2)}, u32[]{:S(2)}) collective-permute-start(bf16[192,1152]{1,0:T(8,128)(2,1)S(1)} %constant_dynamic-slice_fusion.14), channel_id=1, source_target_pairs={{0,8},{4,12},{8,0},{12,4},{16,24},{20,28},{24,16},{28,20},{1,9},{5... | collective-permute-start | bytes 1327112 | tf_op jit(solution)/shard_map/ppermute | solution.py:145
  235.7 28.5 %collective-permute-start.53 = (bf16[320,1152]{1,0:T(8,128)(2,1)S(1)}, bf16[320,1152]{1,0:T(8,128)(2,1)S(1)}, u32[]{:S(2)}, u32[]{:S(2)}) collective-permute-start(bf16[320,1152]{1,0:T(8,128)(2,1)S(1)} %constant_dynamic-slice_fusion.17), channel_id=1, source_target_pairs={{0,4},{4,0},{8,12},{12,8},{16,20},{20,16},{24,28},{28,24},{1,5},{5... | collective-permute-start | bytes 2211848 | tf_op jit(solution)/shard_map/ppermute | solution.py:145
  236.5 67.6 %collective-permute-start.10 = (bf16[512,1024]{1,0:T(8,128)(2,1)S(1)}, bf16[512,1024]{1,0:T(8,128)(2,1)S(1)}, u32[]{:S(2)}, u32[]{:S(2)}) collective-permute-start(bf16[512,1024]{1,0:T(8,128)(2,1)S(1)} %constant_dynamic-slice_fusion.34), channel_id=1, source_target_pairs={{0,1},{1,0},{2,3},{3,2},{4,5},{5,4},{6,7},{7,6},{8,9},{9,8},{10,11... | collective-permute-start | bytes 3145736 | tf_op jit(solution)/shard_map/ppermute | solution.py:145
  236.8 20.6 %collective-permute-start.72 = (bf16[96,1152]{1,0:T(8,128)(2,1)S(1)}, bf16[96,1152]{1,0:T(8,128)(2,1)S(1)}, u32[]{:S(2)}, u32[]{:S(2)}) collective-permute-start(bf16[96,1152]{1,0:T(8,128)(2,1)S(1)} %constant_dynamic-slice_fusion.7), channel_id=1, source_target_pairs={{0,4},{4,0},{8,12},{12,8},{16,20},{20,16},{24,28},{28,24},{1,5},{5... | collective-permute-start | bytes 663560 | tf_op jit(solution)/shard_map/ppermute | solution.py:145
  263.3 41.3 %collective-permute-start.16 = (bf16[512,1024]{1,0:T(8,128)(2,1)S(1)}, bf16[512,1024]{1,0:T(8,128)(2,1)S(1)}, u32[]{:S(2)}, u32[]{:S(2)}) collective-permute-start(bf16[512,1024]{1,0:T(8,128)(2,1)S(1)} %constant_dynamic-slice_fusion.32), channel_id=1, source_target_pairs={{0,1},{1,0},{2,3},{3,2},{4,5},{5,4},{6,7},{7,6},{8,9},{9,8},{10,11... | collective-permute-start | bytes 3145736 | tf_op jit(solution)/shard_map/ppermute | solution.py:145
  263.4 17.3 %collective-permute-start.84 = (bf16[128,1024]{1,0:T(8,128)(2,1)S(1)}, bf16[128,1024]{1,0:T(8,128)(2,1)S(1)}, u32[]{:S(2)}, u32[]{:S(2)}) collective-permute-start(bf16[128,1024]{1,0:T(8,128)(2,1)S(1)} %constant_dynamic-slice_fusion.1), channel_id=1, source_target_pairs={{0,4},{4,0},{8,12},{12,8},{16,20},{20,16},{24,28},{28,24},{1,5},{5... | collective-permute-start | bytes 786440 | tf_op jit(solution)/shard_map/ppermute | solution.py:145
  280.7 20.9 %collective-permute-start.78 = (bf16[160,1024]{1,0:T(8,128)(2,1)S(1)}, bf16[160,1024]{1,0:T(8,128)(2,1)S(1)}, u32[]{:S(2)}, u32[]{:S(2)}) collective-permute-start(bf16[160,1024]{1,0:T(8,128)(2,1)S(1)} %constant_dynamic-slice_fusion.4), channel_id=1, source_target_pairs={{0,8},{4,12},{8,0},{12,4},{16,24},{20,28},{24,16},{28,20},{1,9},{5... | collective-permute-start | bytes 983048 | tf_op jit(solution)/shard_map/ppermute | solution.py:145
  301.6 137.7 %collective-permute-start.7 = (bf16[512,1024]{1,0:T(8,128)(2,1)S(1)}, bf16[512,1024]{1,0:T(8,128)(2,1)S(1)}, u32[]{:S(2)}, u32[]{:S(2)}) collective-permute-start(bf16[512,1024]{1,0:T(8,128)(2,1)S(1)} %constant_dynamic-slice_fusion.35), channel_id=1, source_target_pairs={{0,1},{1,0},{2,3},{3,2},{4,5},{5,4},{6,7},{7,6},{8,9},{9,8},{10,11... | collective-permute-start | bytes 3145736 | tf_op jit(solution)/shard_map/ppermute | solution.py:145
  301.6 23.1 %collective-permute-start.66 = (bf16[160,1152]{1,0:T(8,128)(2,1)S(1)}, bf16[160,1152]{1,0:T(8,128)(2,1)S(1)}, u32[]{:S(2)}, u32[]{:S(2)}) collective-permute-start(bf16[160,1152]{1,0:T(8,128)(2,1)S(1)} %constant_dynamic-slice_fusion.10), channel_id=1, source_target_pairs={{0,8},{4,12},{8,0},{12,4},{16,24},{20,28},{24,16},{28,20},{1,9},{5... | collective-permute-start | bytes 1105928 | tf_op jit(solution)/shard_map/ppermute | solution.py:145
  304.1 32.1 %collective-permute-start.54 = (bf16[160,1152]{1,0:T(8,128)(2,1)S(1)}, bf16[160,1152]{1,0:T(8,128)(2,1)S(1)}, u32[]{:S(2)}, u32[]{:S(2)}) collective-permute-start(bf16[160,1152]{1,0:T(8,128)(2,1)S(1)} %constant_dynamic-slice_fusion.16), channel_id=1, source_target_pairs={{0,8},{4,12},{8,0},{12,4},{16,24},{20,28},{24,16},{28,20},{1,9},{5... | collective-permute-start | bytes 1105928 | tf_op jit(solution)/shard_map/ppermute | solution.py:145
  304.6 18.6 %collective-permute-start.86 = (bf16[64,1024]{1,0:T(8,128)(2,1)S(1)}, bf16[64,1024]{1,0:T(8,128)(2,1)S(1)}, u32[]{:S(2)}, u32[]{:S(2)}) collective-permute-start(bf16[64,1024]{1,0:T(8,128)(2,1)S(1)} %add_convert_fusion.29), channel_id=1, source_target_pairs={{0,16},{4,20},{8,24},{12,28},{16,0},{20,4},{24,8},{28,12},{1,17},{... | collective-permute-start | bytes 393224 | tf_op jit(solution)/shard_map/ppermute | solution.py:145
  324.8 10.3 %collective-permute-start.63 = (bf16[96,1152]{1,0:T(8,128)(2,1)S(1)}, bf16[96,1152]{1,0:T(8,128)(2,1)S(1)}, u32[]{:S(2)}, u32[]{:S(2)}) collective-permute-start(bf16[96,1152]{1,0:T(8,128)(2,1)S(1)} %pad_maximum_fusion.41), channel_id=1, source_target_pairs={{0,4},{4,0},{8,12},{12,8},{16,20},{20,16},{24,28},{28,24},{1,5},{5... | collective-permute-start | bytes 663560 | tf_op jit(solution)/shard_map/ppermute | solution.py:145
  335.0 104.2 %collective-permute-start.11 = (bf16[512,1024]{1,0:T(8,128)(2,1)S(1)}, bf16[512,1024]{1,0:T(8,128)(2,1)S(1)}, u32[]{:S(2)}, u32[]{:S(2)}) collective-permute-start(bf16[512,1024]{1,0:T(8,128)(2,1)S(1)} %add_convert_fusion.8), channel_id=1, source_target_pairs={{0,2},{1,3},{2,0},{3,1},{4,6},{5,7},{6,4},{7,5},{8,10},{9,11},{10,... | collective-permute-start | bytes 3145736 | tf_op jit(solution)/shard_map/ppermute | solution.py:145
  336.2 37.1 %collective-permute-start.87 = (bf16[128,1024]{1,0:T(8,128)(2,1)S(1)}, bf16[128,1024]{1,0:T(8,128)(2,1)S(1)}, u32[]{:S(2)}, u32[]{:S(2)}) collective-permute-start(bf16[128,1024]{1,0:T(8,128)(2,1)S(1)} %pad_maximum_fusion.39), channel_id=1, source_target_pairs={{0,4},{4,0},{8,12},{12,8},{16,20},{20,16},{24,28},{28,24},{1,5},{5... | collective-permute-start | bytes 786440 | tf_op jit(solution)/shard_map/ppermute | solution.py:145
  340.3 10.4 %collective-permute-start.67 = (bf16[80,1152]{1,0:T(8,128)(2,1)S(1)}, bf16[80,1152]{1,0:T(8,128)(2,1)S(1)}, u32[]{:S(2)}, u32[]{:S(2)}) collective-permute-start(bf16[80,1152]{1,0:T(8,128)(2,1)S(1)} %constant_dynamic-slice_fusion.9), channel_id=1, source_target_pairs={{0,16},{4,20},{8,24},{12,28},{16,0},{20,4},{24,8},{28,12},{1,17},{... | collective-permute-start | bytes 552968 | tf_op jit(solution)/shard_map/ppermute | solution.py:145
  350.8 11.8 %collective-permute-start.55 = (bf16[80,1152]{1,0:T(8,128)(2,1)S(1)}, bf16[80,1152]{1,0:T(8,128)(2,1)S(1)}, u32[]{:S(2)}, u32[]{:S(2)}) collective-permute-start(bf16[80,1152]{1,0:T(8,128)(2,1)S(1)} %constant_dynamic-slice_fusion.15), channel_id=1, source_target_pairs={{0,16},{4,20},{8,24},{12,28},{16,0},{20,4},{24,8},{28,12},{1,17},{... | collective-permute-start | bytes 552968 | tf_op jit(solution)/shard_map/ppermute | solution.py:145
  362.6 10.7 %collective-permute-start.80 = (bf16[80,1024]{1,0:T(8,128)(2,1)S(1)}, bf16[80,1024]{1,0:T(8,128)(2,1)S(1)}, u32[]{:S(2)}, u32[]{:S(2)}) collective-permute-start(bf16[80,1024]{1,0:T(8,128)(2,1)S(1)} %add_convert_fusion.27), channel_id=1, source_target_pairs={{0,16},{4,20},{8,24},{12,28},{16,0},{20,4},{24,8},{28,12},{1,17},{... | collective-permute-start | bytes 491528 | tf_op jit(solution)/shard_map/ppermute | solution.py:145
  373.3 20.9 %collective-permute-start.76 = (bf16[192,1152]{1,0:T(8,128)(2,1)S(1)}, bf16[192,1152]{1,0:T(8,128)(2,1)S(1)}, u32[]{:S(2)}, u32[]{:S(2)}) collective-permute-start(bf16[192,1152]{1,0:T(8,128)(2,1)S(1)} %pad_maximum_fusion.34), channel_id=1, source_target_pairs={{0,8},{4,12},{8,0},{12,4},{16,24},{20,28},{24,16},{28,20},{1,9},{5... | collective-permute-start | bytes 1327112 | tf_op jit(solution)/shard_map/ppermute | solution.py:145
  373.3 10.5 %collective-permute-start.68 = (bf16[80,1152]{1,0:T(8,128)(2,1)S(1)}, bf16[80,1152]{1,0:T(8,128)(2,1)S(1)}, u32[]{:S(2)}, u32[]{:S(2)}) collective-permute-start(bf16[80,1152]{1,0:T(8,128)(2,1)S(1)} %add_convert_fusion.25), channel_id=1, source_target_pairs={{0,16},{4,20},{8,24},{12,28},{16,0},{20,4},{24,8},{28,12},{1,17},{... | collective-permute-start | bytes 552968 | tf_op jit(solution)/shard_map/ppermute | solution.py:145
  392.3 13.1 %collective-permute-start.64 = (bf16[192,1152]{1,0:T(8,128)(2,1)S(1)}, bf16[192,1152]{1,0:T(8,128)(2,1)S(1)}, u32[]{:S(2)}, u32[]{:S(2)}) collective-permute-start(bf16[192,1152]{1,0:T(8,128)(2,1)S(1)} %pad_maximum_fusion.33), channel_id=1, source_target_pairs={{0,8},{4,12},{8,0},{12,4},{16,24},{20,28},{24,16},{28,20},{1,9},{5... | collective-permute-start | bytes 1327112 | tf_op jit(solution)/shard_map/ppermute | solution.py:145
  394.2 18.3 %collective-permute-start.81 = (bf16[160,1024]{1,0:T(8,128)(2,1)S(1)}, bf16[160,1024]{1,0:T(8,128)(2,1)S(1)}, u32[]{:S(2)}, u32[]{:S(2)}) collective-permute-start(bf16[160,1024]{1,0:T(8,128)(2,1)S(1)} %pad_maximum_fusion.37), channel_id=1, source_target_pairs={{0,8},{4,12},{8,0},{12,4},{16,24},{20,28},{24,16},{28,20},{1,9},{5... | collective-permute-start | bytes 983048 | tf_op jit(solution)/shard_map/ppermute | solution.py:145
  405.4 15.5 %collective-permute-start.88 = (bf16[256,1024]{1,0:T(8,128)(2,1)S(1)}, bf16[256,1024]{1,0:T(8,128)(2,1)S(1)}, u32[]{:S(2)}, u32[]{:S(2)}) collective-permute-start(bf16[256,1024]{1,0:T(8,128)(2,1)S(1)} %pad_maximum_fusion.31), channel_id=1, source_target_pairs={{0,8},{4,12},{8,0},{12,4},{16,24},{20,28},{24,16},{28,20},{1,9},{5... | collective-permute-start | bytes 1572872 | tf_op jit(solution)/shard_map/ppermute | solution.py:145
  412.5 14.5 %collective-permute-start.69 = (bf16[160,1152]{1,0:T(8,128)(2,1)S(1)}, bf16[160,1152]{1,0:T(8,128)(2,1)S(1)}, u32[]{:S(2)}, u32[]{:S(2)}) collective-permute-start(bf16[160,1152]{1,0:T(8,128)(2,1)S(1)} %pad_maximum_fusion.36), channel_id=1, source_target_pairs={{0,8},{4,12},{8,0},{12,4},{16,24},{20,28},{24,16},{28,20},{1,9},{5... | collective-permute-start | bytes 1105928 | tf_op jit(solution)/shard_map/ppermute | solution.py:145
  420.9 15.9 %collective-permute-start.17 = (bf16[512,1024]{1,0:T(8,128)(2,1)S(1)}, bf16[512,1024]{1,0:T(8,128)(2,1)S(1)}, u32[]{:S(2)}, u32[]{:S(2)}) collective-permute-start(bf16[512,1024]{1,0:T(8,128)(2,1)S(1)} %add_convert_fusion.7), channel_id=1, source_target_pairs={{0,2},{1,3},{2,0},{3,1},{4,6},{5,7},{6,4},{7,5},{8,10},{9,11},{10,... | collective-permute-start | bytes 3145736 | tf_op jit(solution)/shard_map/ppermute | solution.py:145
  434.5 17.7 %collective-permute-start.82 = (bf16[320,1024]{1,0:T(8,128)(2,1)S(1)}, bf16[320,1024]{1,0:T(8,128)(2,1)S(1)}, u32[]{:S(2)}, u32[]{:S(2)}) collective-permute-start(bf16[320,1024]{1,0:T(8,128)(2,1)S(1)} %pad_maximum_fusion.26), channel_id=1, source_target_pairs={{0,4},{4,0},{8,12},{12,8},{16,20},{20,16},{24,28},{28,24},{1,5},{5... | collective-permute-start | bytes 1966088 | tf_op jit(solution)/shard_map/ppermute | solution.py:145
  436.2 29.3 %collective-permute-start.70 = (bf16[320,1152]{1,0:T(8,128)(2,1)S(1)}, bf16[320,1152]{1,0:T(8,128)(2,1)S(1)}, u32[]{:S(2)}, u32[]{:S(2)}) collective-permute-start(bf16[320,1152]{1,0:T(8,128)(2,1)S(1)} %pad_maximum_fusion.25), channel_id=1, source_target_pairs={{0,4},{4,0},{8,12},{12,8},{16,20},{20,16},{24,28},{28,24},{1,5},{5... | collective-permute-start | bytes 2211848 | tf_op jit(solution)/shard_map/ppermute | solution.py:145
  436.8 36.6 %collective-permute-start.58 = (bf16[320,1152]{1,0:T(8,128)(2,1)S(1)}, bf16[320,1152]{1,0:T(8,128)(2,1)S(1)}, u32[]{:S(2)}, u32[]{:S(2)}) collective-permute-start(bf16[320,1152]{1,0:T(8,128)(2,1)S(1)} %pad_maximum_fusion.24), channel_id=1, source_target_pairs={{0,4},{4,0},{8,12},{12,8},{16,20},{20,16},{24,28},{28,24},{1,5},{5... | collective-permute-start | bytes 2211848 | tf_op jit(solution)/shard_map/ppermute | solution.py:145
  443.8 32.6 %collective-permute-start.18 = (bf16[512,1024]{1,0:T(8,128)(2,1)S(1)}, bf16[512,1024]{1,0:T(8,128)(2,1)S(1)}, u32[]{:S(2)}, u32[]{:S(2)}) collective-permute-start(bf16[512,1024]{1,0:T(8,128)(2,1)S(1)} %get-tuple-element.38), channel_id=1, source_target_pairs={{0,1},{1,0},{2,3},{3,2},{4,5},{5,4},{6,7},{7,6},{8,9},{9,8},{10,11... | collective-permute-start | bytes 3145736 | tf_op jit(solution)/shard_map/ppermute | solution.py:145
  443.8 30.0 %collective-permute-start.20 = (bf16[512,1024]{1,0:T(8,128)(2,1)S(1)}, bf16[512,1024]{1,0:T(8,128)(2,1)S(1)}, u32[]{:S(2)}, u32[]{:S(2)}) collective-permute-start(bf16[512,1024]{1,0:T(8,128)(2,1)S(1)} %get-tuple-element.38), channel_id=1, source_target_pairs={{0,2},{1,3},{2,0},{3,1},{4,6},{5,7},{6,4},{7,5},{8,10},{9,11},{10,... | collective-permute-start | bytes 3145736 | tf_op jit(solution)/shard_map/ppermute | solution.py:145
  501.2 82.6 %collective-permute-start.19 = (bf16[512,1024]{1,0:T(8,128)(2,1)S(1)}, bf16[512,1024]{1,0:T(8,128)(2,1)S(1)}, u32[]{:S(2)}, u32[]{:S(2)}) collective-permute-start(bf16[512,1024]{1,0:T(8,128)(2,1)S(1)} %constant_dynamic-slice_fusion.31), channel_id=1, source_target_pairs={{0,1},{1,0},{2,3},{3,2},{4,5},{5,4},{6,7},{7,6},{8,9},{9,8},{10,11... | collective-permute-start | bytes 3145736 | tf_op jit(solution)/shard_map/ppermute | solution.py:145
  502.7 64.5 %collective-permute-start.22 = (bf16[512,1024]{1,0:T(8,128)(2,1)S(1)}, bf16[512,1024]{1,0:T(8,128)(2,1)S(1)}, u32[]{:S(2)}, u32[]{:S(2)}) collective-permute-start(bf16[512,1024]{1,0:T(8,128)(2,1)S(1)} %constant_dynamic-slice_fusion.30), channel_id=1, source_target_pairs={{0,1},{1,0},{2,3},{3,2},{4,5},{5,4},{6,7},{7,6},{8,9},{9,8},{10,11... | collective-permute-start | bytes 3145736 | tf_op jit(solution)/shard_map/ppermute | solution.py:145
  503.2 51.3 %collective-permute-start.24 = (bf16[320,768]{1,0:T(8,128)(2,1)S(1)}, bf16[320,768]{1,0:T(8,128)(2,1)S(1)}, u32[]{:S(2)}, u32[]{:S(2)}) collective-permute-start(bf16[320,768]{1,0:T(8,128)(2,1)S(1)} %constant_dynamic-slice_fusion.29), channel_id=1, source_target_pairs={{0,4},{4,0},{8,12},{12,8},{16,20},{20,16},{24,28},{28,24},{1,5},{5... | collective-permute-start | bytes 1474568 | tf_op jit(solution)/shard_map/ppermute | solution.py:145
  504.9 34.8 %collective-permute-start.30 = (bf16[192,768]{1,0:T(8,128)(2,1)S(1)}, bf16[192,768]{1,0:T(8,128)(2,1)S(1)}, u32[]{:S(2)}, u32[]{:S(2)}) collective-permute-start(bf16[192,768]{1,0:T(8,128)(2,1)S(1)} %constant_dynamic-slice_fusion.26), channel_id=1, source_target_pairs={{0,8},{4,12},{8,0},{12,4},{16,24},{20,28},{24,16},{28,20},{1,9},{5... | collective-permute-start | bytes 884744 | tf_op jit(solution)/shard_map/ppermute | solution.py:145
  564.3 12.3 %collective-permute-start.34 = (bf16[96,768]{1,0:T(8,128)(2,1)S(1)}, bf16[96,768]{1,0:T(8,128)(2,1)S(1)}, u32[]{:S(2)}, u32[]{:S(2)}) collective-permute-start(bf16[96,768]{1,0:T(8,128)(2,1)S(1)} %pad_maximum_fusion.43), channel_id=1, source_target_pairs={{0,4},{4,0},{8,12},{12,8},{16,20},{20,16},{24,28},{28,24},{1,5},{5... | collective-permute-start | bytes 442376 | tf_op jit(solution)/shard_map/ppermute | solution.py:145
  567.6 16.3 %collective-permute-start.23 = (bf16[512,1024]{1,0:T(8,128)(2,1)S(1)}, bf16[512,1024]{1,0:T(8,128)(2,1)S(1)}, u32[]{:S(2)}, u32[]{:S(2)}) collective-permute-start(bf16[512,1024]{1,0:T(8,128)(2,1)S(1)} %add_convert_fusion.6), channel_id=1, source_target_pairs={{0,2},{1,3},{2,0},{3,1},{4,6},{5,7},{6,4},{7,5},{8,10},{9,11},{10,... | collective-permute-start | bytes 3145736 | tf_op jit(solution)/shard_map/ppermute | solution.py:145
  (106 other events, 837.4 us)

commit v2 on v1

--- a/solution.py
+++ b/solution.py
@@ -156,27 +156,68 @@
     )
 
 
-def halving(values, order):
-    place = lax.axis_index("dp")
-    piece = values.astype(jnp.bfloat16)
-    for step in order:
-        bit = (place // step) % 2
-        arrived = swap(part(piece, 1 - bit), "dp", step)
-        piece = (
-            part(piece, bit).astype(jnp.float32) + arrived.astype(jnp.float32)
-        ).astype(jnp.bfloat16)
-    for step in reversed(order):
-        bit = (place // step) % 2
-        piece = in_order(bit, piece, swap(piece, "dp", step))
-    return piece
-
-
-def dp_sum(values):
-    rows = values.shape[0]
-    cut = max(rows * 5 // 8 // 128, 1) * 128
-    return jnp.concatenate(
-        [halving(values[:cut], (1, 2, 4)), halving(values[cut:], (2, 1, 4))], axis=0
-    ).astype(jnp.float32)
+def tied(values, after):
+    return lax.optimization_barrier((values, after))[0]
+
+
+class Sum:
+    def __init__(self, values):
+        rows = values.shape[0]
+        cut = max(rows * 5 // 8 // 128, 1) * 128
+        low = values.astype(jnp.bfloat16)
+        self.place = lax.axis_index("dp")
+        self.pieces = [low[:cut], low[cut:]]
+        self.sent = None
+        self.stage = 0
+        self.start()
+
+    def bit(self, step):
+        return (self.place // step) % 2
+
+    def steps(self):
+        return {0: (1, 2), 1: (2, 1), 2: (4,), 3: (4,), 4: (2, 1), 5: (1, 2)}[self.stage]
+
+    def start(self):
+        steps = self.steps()
+        if self.stage == 2:
+            self.pieces = [jnp.concatenate(self.pieces, axis=0)]
+        out = self.pieces
+        if self.stage < 3:
+            out = [part(p, 1 - self.bit(step)) for p, step in zip(out, steps)]
+        self.sent = [swap(p, "dp", step) for p, step in zip(out, steps)]
+
+    def advance(self, after=None):
+        steps = self.steps()
+        arrived = self.sent
+        if after is not None:
+            arrived = tied(arrived, after)
+        if self.stage < 3:
+            self.pieces = [
+                (
+                    part(p, self.bit(step)).astype(jnp.float32) + got.astype(jnp.float32)
+                ).astype(jnp.bfloat16)
+                for p, got, step in zip(self.pieces, arrived, steps)
+            ]
+        else:
+            self.pieces = [
+                in_order(self.bit(step), p, got)
+                for p, got, step in zip(self.pieces, arrived, steps)
+            ]
+        if self.stage == 2:
+            self.cut = self.sizes[0]
+        if self.stage == 3:
+            whole = self.pieces[0]
+            self.pieces = [whole[: self.cut], whole[self.cut :]]
+        if self.stage == 1:
+            self.sizes = [p.shape[0] for p in self.pieces]
+        self.stage += 1
+        if self.stage < 6:
+            self.start()
+
+    def finish(self):
+        while self.stage < 6:
+            self.advance()
+        return jnp.concatenate(self.pieces, axis=0).astype(jnp.float32)
 
 
 def small_sum(values, axis):
@@ -196,11 +237,13 @@
     return near, far, across
 
 
+def sum_far(far, core):
+    arrived = swap(part(far, 1 - core), "tensor", 1)
+    return (part(far, core).astype(jnp.float32) + arrived.astype(jnp.float32)).astype(jnp.bfloat16)
+
+
 def reduce_far(far, core):
-    low = jnp.bfloat16
-    arrived = swap(part(far, 1 - core), "tensor", 1)
-    total = (part(far, core).astype(jnp.float32) + arrived.astype(jnp.float32)).astype(low)
-    return swap(total, "tensor", 2)
+    return swap(sum_far(far, core), "tensor", 2)
 
 
 def reduce_near(near, core, crossed):
@@ -295,30 +338,69 @@
     cot_near, cot_far, _ = gather_pair(cotangent, core, after=two_across)
     hidden_near, mlp_near = mlp_forward(two_near, w_gate, w_up)
     gate_near, up_near, back_near = mlp_backward(cot_near, mlp_near, w_gate, w_up, w_down)
-    hidden_far, mlp_far = mlp_forward(two_far, w_gate, w_up)
-    out_crossed = reduce_far(dot(hidden_far, w_down).astype(low), core)
-    gate_far, up_far, back_far = mlp_backward(cot_far, mlp_far, w_gate, w_up, w_down)
-    back_crossed = reduce_far(back_far, core)
-    grad_down = dp_sum(dot_first(hidden_near, cot_near) + dot_first(hidden_far, cot_far))
-    grad_wgate = dp_sum(dot_first(two_near, gate_near) + dot_first(two_far, gate_far))
-    grad_wup = dp_sum(dot_first(two_near, up_near) + dot_first(two_far, up_far))
-    result = resid + reduce_near(dot(hidden_near, w_down).astype(low), core, out_crossed)
-    back_rows = reduce_near(back_near, core, back_crossed)
+    hidden_far, mlp_far = mlp_forward(tied(two_far, back_near), w_gate, w_up)
+    grad_down = (dot_first(hidden_near, cot_near) + dot_first(hidden_far, cot_far)).astype(low)
+    sum_down = Sum(grad_down)
+    gate_far, up_far, back_far = mlp_backward(
+        tied(cot_far, grad_down), mlp_far, w_gate, w_up, w_down
+    )
+    back_sum = sum_far(back_far, core)
+    back_crossed = swap(back_sum, "tensor", 2)
+    sum_down.advance(after=back_sum)
+    grad_gate = (dot_first(two_near, gate_near) + dot_first(two_far, gate_far)).astype(low)
+    sum_gate = Sum(grad_gate)
+    grad_up = (dot_first(two_near, up_near) + dot_first(two_far, up_far)).astype(low)
+    sum_up = Sum(grad_up)
+    back_rows = reduce_near(back_near, core, tied(back_crossed, grad_up))
     grad_resid = cotangent.astype(jnp.float32) + norm_back(back_rows, unit_two, scale_two, gain_mlp)
     gain_two = jnp.sum(back_rows * unit_two, axis=0)
-    gm_near, gm_far, _ = gather_pair(grad_resid.astype(low), core)
+    grad_mixed = grad_resid.astype(low)
+    gm_near, gm_far, _ = gather_pair(grad_mixed, core)
+    sum_down.advance(after=grad_mixed)
+    sum_gate.advance(after=grad_mixed)
+    out_crossed = reduce_far(dot(hidden_far, w_down).astype(low), core)
     gp_near, taps_near = conv_backward(gm_near, kept_near, w_out, taps)
+    first_near = dot_last(gp_near, in_flat).astype(low)
+    sum_down.advance(after=first_near)
+    sum_up.advance(after=first_near)
     gp_far, taps_far = conv_backward(gm_far, kept_far, w_out, taps)
-    first_crossed = reduce_far(dot_last(gp_far, in_flat).astype(low), core)
-    grad_wout = dp_sum(dot_first(mixed_near, gm_near) + dot_first(mixed_far, gm_far))
-    grad_win = dp_sum(dot_first(one_near, gp_near) + dot_first(one_far, gp_far))
-    back_first = reduce_near(dot_last(gp_near, in_flat).astype(low), core, first_crossed)
+    first_sum = sum_far(dot_last(gp_far, in_flat).astype(low), core)
+    first_crossed = swap(first_sum, "tensor", 2)
+    grad_conv = jnp.concatenate(
+        [
+            dot_first(one_near, gp_near) + dot_first(one_far, gp_far),
+            dot_first(gm_near, mixed_near) + dot_first(gm_far, mixed_far),
+        ],
+        axis=1,
+    ).astype(low)
+    sum_conv = Sum(grad_conv)
+    sum_gate.advance(after=first_sum)
+    sum_down.advance(after=first_sum)
+    sum_up.advance(after=grad_conv)
+    result = resid + reduce_near(dot(hidden_near, w_down).astype(low), core, out_crossed)
+    back_first = reduce_near(first_near, core, first_crossed)
     gain_one = jnp.sum(back_first * unit_one, axis=0)
     grad_tokens = grad_resid + norm_back(back_first, unit_one, scale_one, gain_mix)
     gains = small_sum(jnp.stack([gain_one, gain_two]), "tensor")
     small = small_sum(
         jnp.concatenate([gains.reshape(-1), (taps_near + taps_far).reshape(-1)]), "dp"
     )
+    sum_conv.advance()
+    sum_down.advance(after=sum_conv.pieces[0])
+    sum_gate.advance(after=sum_conv.pieces[0])
+    sum_up.advance(after=sum_conv.pieces[0])
+    sum_conv.advance()
+    sum_gate.advance(after=sum_conv.pieces[0])
+    sum_up.advance(after=sum_conv.pieces[0])
+    grad_down = sum_down.finish()
+    sum_conv.advance()
+    sum_gate.advance(after=sum_conv.pieces[0])
+    sum_up.advance(after=sum_conv.pieces[0])
+    grad_wgate = sum_gate.finish()
+    grad_wup = sum_up.finish()
+    grad_conv = sum_conv.finish()
+    grad_win = grad_conv[:, : 3 * channels]
+    grad_wout = grad_conv[:, 3 * channels :].T
     return (
         result,
         grad_tokens,

time: 617 us -> 557 us (0.903)
  waiting for transfers between devices: 321 us -> 268 us
  starting transfers between devices: 85.4 us -> 72.3 us
  matrix products: 121 us -> 113 us
  local copies, waits for them, and re-layouts: 29.3 us -> 36.5 us
    ppermute x89 -> x69, waiting for transfers between devices: 321 us -> 268 us  [swap(): return lax.ppermute(values, axis, [(i, i ^ step) for i in range(count)])]
    ppermute x89 -> x69, starting transfers between devices: 85.4 us -> 72.3 us  [swap(): return lax.ppermute(values, axis, [(i, i ^ step) for i in range(count)])]
    dot_general x10, matrix products: 45.5 us -> 33.8 us  [dot(): return jnp.dot(left, right, preferred_element_type=jnp.float32)]
    dot_general x10, matrix products: 34.9 us -> 42 us  [dot_first(): lax.dot_general(left, right, (((0,), (0,)), ((), ())), preferred_element_...]
    select_n x38 -> x28, other arithmetic: 13 us -> 16.9 us  [in_order(): jnp.where(bit == 0, mine, other)]
    unnamed x133 -> x162, local copies, waits for them, and re-layouts: 19.9 us -> 21.9 us
    convert_element_type x40 -> x29, other arithmetic: 22.7 us -> 23.3 us  [the longest x20 8.42 us: advance(): self.pieces = [(part(p, self.bit(step)).astype(jnp.float32) + got.astype(...]
  transfers between devices with their start and end apart: 89 -> 69, of which waited for: 48 -> 30; matrix products, arithmetic and copies ran while one was open for 26% -> 32% of each run, Pallas kernels for 0% -> 0%
where the time goes in v2:
time: 557 us; the launch traced here: 551 us
  waiting for transfers between devices  268 us (48%)
  matrix products  113 us (20%)
  starting transfers between devices  72.3 us (13%)
  other arithmetic  58 us (10%)
  local copies, waits for them, and re-layouts  36.5 us (7%)
    ppermute x69, waiting for transfers between devices, swap(): return lax.ppermute(values, axis, [(i, i ^ step) for i in range(count)])  268 us
    ppermute x69, starting transfers between devices, swap(): return lax.ppermute(values, axis, [(i, i ^ step) for i in range(count)])  72.3 us
    dot_general x10, matrix products, dot_first(): lax.dot_general(left, right, (((0,), (0,)), ((), ())), preferred_element_...  42 us
    dot_general x10, matrix products, dot_last(): lax.dot_general(left, right, (((1,), (1,)), ((), ())), preferred_element_...  37.6 us
    dot_general x10, matrix products, dot(): return jnp.dot(left, right, preferred_element_type=jnp.float32)  33.8 us
    unnamed x162, local copies, waits for them, and re-layouts  21.9 us
    select_n x28, other arithmetic, in_order(): jnp.where(bit == 0, mine, other)  16.9 us
  transfers between devices with their start and end apart: 69, of which 30 were waited for; matrix products, arithmetic and copies ran while one was open for 32% of the time, Pallas kernels for 0%

profile of v2, /device:TPU:0, one launch (start us, length us, event | category | flops | bytes accessed | tf_op | source)
XLA Modules:
  0.0 551.1 jit_solution(230157736943544655)
XLA Ops:
  4.8 2.9 collective-permute-start.2
  7.8 23.5 %collective-permute-done.2 = bf16[512,1024]{1,0:T(8,128)(2,1)} collective-permute-done((bf16[512,1024]{1,0:T(8,128)(2,1)}, bf16[512,1024]{1,0:T(8,128)(2,1)}, u32[]{:S(2)}, u32[]{:S(2)}) %collective-permute-start.2) | collective-permute-done | bytes 1048608 | tf_op jit(solution)/shard_map/ppermute | solution.py:145
  55.8 23.6 %collective-permute-done.5 = bf16[512,1024]{1,0:T(8,128)(2,1)S(1)} collective-permute-done((bf16[512,1024]{1,0:T(8,128)(2,1)S(1)}, bf16[512,1024]{1,0:T(8,128)(2,1)S(1)}, u32[]{:S(2)}, u32[]{:S(2)}) %collective-permute-start.5) | collective-permute-done | bytes 1048608 | tf_op jit(solution)/shard_map/ppermute | solution.py:145
  84.2 5.5 %fusion.15 = f32[1024,1152]{1,0:T(8,128)} fusion(bf16[1152,1024]{1,0:T(8,128)(2,1)S(1)} %copy-done.69, bf16[512,1024]{1,0:T(8,128)(2,1)S(1)} %get-tuple-element.123, bf16[512,1024]{1,0:T(8,128)(2,1)S(1)} %get-tuple-element.122), kind=kOutput, calls=%fused_computation.72 | convolution fusion | flops 2420113408 | bytes 9175040 | tf_op jit(solution)/shard_map/dot_general | solution.py:37
  93.3 2.9 fusion.54
  96.2 8.4 %multiply_convert_fusion.5 = (bf16[1024,1152]{1,0:T(8,128)(2,1)}, bf16[1024,1152]{1,0:T(8,128)(2,1)S(1)}, bf16[1024,1152]{1,0:T(8,128)(2,1)}) fusion(f32[1024,1152]{1,0:T(8,128)S(1)} %fusion.54, f32[1024,1152]{1,0:T(8,128)} %fusion.15, bf16[1024,1152]{1,0:T(8,128)(2,1)S(1)} %copy-done, bf16[512,1024]{1,0:T(8,128)(2,1)S(1)} %get-tuple-element.125, ...), kind=kOutput, calls=%fused_computation.9 | convolution fusion | flops 2438987776 | bytes 20971520 | tf_op jit(solution)/shard_map/dot_general | solution.py:259
  104.5 5.6 %convolution_convert_fusion.1 = bf16[1024,1024]{1,0:T(8,128)(2,1)S(1)} fusion(bf16[1024,1152]{1,0:T(8,128)(2,1)} %get-tuple-element.112, bf16[1152,1024]{1,0:T(8,128)(2,1)S(1)} %copy-done.69), kind=kOutput, calls=%fused_computation.58 | convolution fusion | flops 2416967680 | bytes 6815744 | tf_op jit(solution)/shard_map/dot_general | solution.py:259
  112.9 2.9 fusion.60
  116.9 4.8 add_convert_fusion.4
  123.4 16.0 %fusion.52 = f32[1024,1152]{1,0:T(8,128)} fusion(bf16[1024,1152]{1,0:T(8,128)(2,1)S(1)} %copy-done.76, bf16[512,1024]{1,0:T(8,128)(2,1)S(1)} %get-tuple-element.125, bf16[512,1024]{1,0:T(8,128)(2,1)S(1)} %get-tuple-element.124), kind=kOutput, calls=%fused_computation.274 | convolution fusion | flops 2420113408 | bytes 9175040 | tf_op jit(solution)/shard_map/dot_general | solution.py:31
  139.4 4.6 fusion.51
  144.4 2.9 fusion.61
  147.3 4.5 multiply_convert_fusion.2
  151.9 3.1 convolution_convert_fusion
  155.9 2.9 add_convert_fusion.2
  159.0 8.7 %multiply_convert_fusion = (bf16[1024,1152]{1,0:T(8,128)(2,1)}, bf16[1024,1152]{1,0:T(8,128)(2,1)}) fusion(f32[1024,1152]{1,0:T(8,128)} %copy-done.71, f32[1024,1152]{1,0:T(8,128)} %get-tuple-element.184, bf16[1024,1024]{1,0:T(8,128)(2,1)S(1)} %pad_maximum_fusion.6, bf16[1152,1024]{1,0:T(8,128)(2,1)} %param.16), kind=kOutput, calls=%fused_computation.2 | convolution fusion | flops 2431254528 | bytes 18612224 | tf_op jit(solution)/shard_map/dot_general | solution.py:37
  167.7 5.4 fusion.62
  173.1 3.1 add_convert_fusion.3
  178.1 4.9 add_convert_fusion.1
  183.0 5.2 add_convert_fusion
  194.3 9.4 %collective-permute-done.60 = bf16[256,1024]{1,0:T(8,128)(2,1)S(1)} collective-permute-done((bf16[256,1024]{1,0:T(8,128)(2,1)S(1)}, bf16[256,1024]{1,0:T(8,128)(2,1)S(1)}, u32[]{:S(2)}, u32[]{:S(2)}) %collective-permute-start.60) | collective-permute-done | bytes 524320 | tf_op jit(solution)/shard_map/ppermute | solution.py:145
  206.8 11.9 %collective-permute-done.17 = bf16[512,1024]{1,0:T(8,128)(2,1)S(1)} collective-permute-done((bf16[512,1024]{1,0:T(8,128)(2,1)S(1)}, bf16[512,1024]{1,0:T(8,128)(2,1)S(1)}, u32[]{:S(2)}, u32[]{:S(2)}) %collective-permute-start.17) | collective-permute-done | bytes 1048608 | tf_op jit(solution)/shard_map/ppermute | solution.py:145
  223.1 17.1 %collective-permute-done.12 = bf16[512,1024]{1,0:T(8,128)(2,1)S(1)} collective-permute-done((bf16[512,1024]{1,0:T(8,128)(2,1)S(1)}, bf16[512,1024]{1,0:T(8,128)(2,1)S(1)}, u32[]{:S(2)}, u32[]{:S(2)}) %collective-permute-start.12) | collective-permute-done | bytes 1048608 | tf_op jit(solution)/shard_map/ppermute | solution.py:145
  240.6 3.8 fusion.57
  244.4 12.4 %collective-permute-done.62 = bf16[128,1024]{1,0:T(8,128)(2,1)S(1)} collective-permute-done((bf16[128,1024]{1,0:T(8,128)(2,1)S(1)}, bf16[128,1024]{1,0:T(8,128)(2,1)S(1)}, u32[]{:S(2)}, u32[]{:S(2)}) %collective-permute-start.62) | collective-permute-done | bytes 262176 | tf_op jit(solution)/shard_map/ppermute | solution.py:145
  258.7 7.2 %collective-permute-done.40 = bf16[192,1152]{1,0:T(8,128)(2,1)S(1)} collective-permute-done((bf16[192,1152]{1,0:T(8,128)(2,1)S(1)}, bf16[192,1152]{1,0:T(8,128)(2,1)S(1)}, u32[]{:S(2)}, u32[]{:S(2)}) %collective-permute-start.40) | collective-permute-done | bytes 442400 | tf_op jit(solution)/shard_map/ppermute | solution.py:145
  269.7 9.6 %collective-permute-done.20 = bf16[512,1024]{1,0:T(8,128)(2,1)S(1)} collective-permute-done((bf16[512,1024]{1,0:T(8,128)(2,1)S(1)}, bf16[512,1024]{1,0:T(8,128)(2,1)S(1)}, u32[]{:S(2)}, u32[]{:S(2)}) %collective-permute-start.20) | collective-permute-done | bytes 1048608 | tf_op jit(solution)/shard_map/ppermute | solution.py:145
  306.2 3.1 convolution_convert_fusion.4
  320.1 8.4 %collective-permute-done.51 = bf16[160,1152]{1,0:T(8,128)(2,1)} collective-permute-done((bf16[160,1152]{1,0:T(8,128)(2,1)}, bf16[160,1152]{1,0:T(8,128)(2,1)}, u32[]{:S(2)}, u32[]{:S(2)}) %collective-permute-start.51) | collective-permute-done | bytes 368672 | tf_op jit(solution)/shard_map/ppermute | solution.py:145
  330.6 8.9 %collective-permute-done.26 = bf16[192,1024]{1,0:T(8,128)(2,1)S(1)} collective-permute-done((bf16[192,1024]{1,0:T(8,128)(2,1)S(1)}, bf16[192,1024]{1,0:T(8,128)(2,1)S(1)}, u32[]{:S(2)}, u32[]{:S(2)}) %collective-permute-start.26) | collective-permute-done | bytes 393248 | tf_op jit(solution)/shard_map/ppermute | solution.py:145
  340.8 4.9 collective-permute-done.27
  348.7 13.8 %collective-permute-done.53 = bf16[128,1152]{1,0:T(8,128)(2,1)S(1)} collective-permute-done((bf16[128,1152]{1,0:T(8,128)(2,1)S(1)}, bf16[128,1152]{1,0:T(8,128)(2,1)S(1)}, u32[]{:S(2)}, u32[]{:S(2)}) %collective-permute-start.53) | collective-permute-done | bytes 294944 | tf_op jit(solution)/shard_map/ppermute | solution.py:145
  363.3 8.6 %collective-permute-done.25 = bf16[160,1024]{1,0:T(8,128)(2,1)S(1)} collective-permute-done((bf16[160,1024]{1,0:T(8,128)(2,1)S(1)}, bf16[160,1024]{1,0:T(8,128)(2,1)S(1)}, u32[]{:S(2)}, u32[]{:S(2)}) %collective-permute-start.25) | collective-permute-done | bytes 327712 | tf_op jit(solution)/shard_map/ppermute | solution.py:145
  374.4 12.8 %collective-permute-done.54 = bf16[128,1152]{1,0:T(8,128)(2,1)S(1)} collective-permute-done((bf16[128,1152]{1,0:T(8,128)(2,1)S(1)}, bf16[128,1152]{1,0:T(8,128)(2,1)S(1)}, u32[]{:S(2)}, u32[]{:S(2)}) %collective-permute-start.54) | collective-permute-done | bytes 294944 | tf_op jit(solution)/shard_map/ppermute | solution.py:145
  389.7 3.4 collective-permute-start.28
  396.6 6.3 %collective-permute-done.28 = bf16[128,1024]{1,0:T(8,128)(2,1)S(1)} collective-permute-done((bf16[128,1024]{1,0:T(8,128)(2,1)S(1)}, bf16[128,1024]{1,0:T(8,128)(2,1)S(1)}, u32[]{:S(2)}, u32[]{:S(2)}) %collective-permute-start.28) | collective-permute-done | bytes 262176 | tf_op jit(solution)/shard_map/ppermute | solution.py:145
  404.1 13.7 %collective-permute-done.43 = bf16[128,1152]{1,0:T(8,128)(2,1)S(1)} collective-permute-done((bf16[128,1152]{1,0:T(8,128)(2,1)S(1)}, bf16[128,1152]{1,0:T(8,128)(2,1)S(1)}, u32[]{:S(2)}, u32[]{:S(2)}) %collective-permute-start.43) | collective-permute-done | bytes 294944 | tf_op jit(solution)/shard_map/ppermute | solution.py:145
  419.2 2.9 collective-permute-start.29
  422.4 3.3 collective-permute-done.66
  428.4 4.1 collective-permute-done.65
  434.0 5.1 collective-permute-done.29
  439.9 5.9 %collective-permute-done.44 = bf16[128,1152]{1,0:T(8,128)(2,1)S(1)} collective-permute-done((bf16[128,1152]{1,0:T(8,128)(2,1)S(1)}, bf16[128,1152]{1,0:T(8,128)(2,1)S(1)}, u32[]{:S(2)}, u32[]{:S(2)}) %collective-permute-start.44) | collective-permute-done | bytes 294944 | tf_op jit(solution)/shard_map/ppermute | solution.py:145
  446.9 6.7 %collective-permute-done.32 = bf16[96,1024]{1,0:T(8,128)(2,1)S(1)} collective-permute-done((bf16[96,1024]{1,0:T(8,128)(2,1)S(1)}, bf16[96,1024]{1,0:T(8,128)(2,1)S(1)}, u32[]{:S(2)}, u32[]{:S(2)}) %collective-permute-start.32) | collective-permute-done | bytes 196640 | tf_op jit(solution)/shard_map/ppermute | solution.py:145
  456.1 17.1 %collective-permute-done.30 = bf16[160,1024]{1,0:T(8,128)(2,1)S(1)} collective-permute-done((bf16[160,1024]{1,0:T(8,128)(2,1)S(1)}, bf16[160,1024]{1,0:T(8,128)(2,1)S(1)}, u32[]{:S(2)}, u32[]{:S(2)}) %collective-permute-start.30) | collective-permute-done | bytes 327712 | tf_op jit(solution)/shard_map/ppermute | solution.py:145
  476.6 4.9 collective-permute-done.46
  486.9 9.3 %collective-permute-done.67 = bf16[320,1024]{1,0:T(8,128)(2,1)S(1)} collective-permute-done((bf16[320,1024]{1,0:T(8,128)(2,1)S(1)}, bf16[320,1024]{1,0:T(8,128)(2,1)S(1)}, u32[]{:S(2)}, u32[]{:S(2)}) %collective-permute-start.67) | collective-permute-done | bytes 655392 | tf_op jit(solution)/shard_map/ppermute | solution.py:145
  510.8 14.5 %collective-permute-done.36 = f32[2816]{0:T(1024)S(1)} collective-permute-done((f32[2816]{0:T(1024)S(1)}, f32[2816]{0:T(1024)S(1)}, u32[]{:S(2)}, u32[]{:S(2)}) %collective-permute-start.36) | collective-permute-done | bytes 11296 | tf_op jit(solution)/shard_map/ppermute | solution.py:145
  543.3 3.6 copy.32
  (425 shorter events, 173.9 us)
Async XLA Ops:
  4.8 26.4 %collective-permute-start.2 = (bf16[512,1024]{1,0:T(8,128)(2,1)}, bf16[512,1024]{1,0:T(8,128)(2,1)}, u32[]{:S(2)}, u32[]{:S(2)}) collective-permute-start(bf16[512,1024]{1,0:T(8,128)(2,1)} %fusion.4), channel_id=1, source_target_pairs={{0,2},{1,3},{2,0},{3,1},{4,6},{5,7},{6,4},{7,5},{8,10},{9,11},{10,... | collective-permute-start | bytes 3145736 | tf_op jit(solution)/shard_map/ppermute | solution.py:145
  7.8 26.1 %collective-permute-start = (bf16[512,1024]{1,0:T(8,128)(2,1)}, bf16[512,1024]{1,0:T(8,128)(2,1)}, u32[]{:S(2)}, u32[]{:S(2)}) collective-permute-start(bf16[512,1024]{1,0:T(8,128)(2,1)} %fusion.4), channel_id=1, source_target_pairs={{0,1},{1,0},{2,3},{3,2},{4,5},{5,4},{6,7},{7,6},{8,9},{9,8},{10,11... | collective-permute-start | bytes 3145736 | tf_op jit(solution)/shard_map/ppermute | solution.py:145
  53.9 25.5 %collective-permute-start.5 = (bf16[512,1024]{1,0:T(8,128)(2,1)S(1)}, bf16[512,1024]{1,0:T(8,128)(2,1)S(1)}, u32[]{:S(2)}, u32[]{:S(2)}) collective-permute-start(bf16[512,1024]{1,0:T(8,128)(2,1)S(1)} %add_convert_fusion.9), channel_id=1, source_target_pairs={{0,2},{1,3},{2,0},{3,1},{4,6},{5,7},{6,4},{7,5},{8,10},{9,11},{10,... | collective-permute-start | bytes 3145736 | tf_op jit(solution)/shard_map/ppermute | solution.py:145
  55.7 26.2 %collective-permute-start.10 = (bf16[512,1024]{1,0:T(8,128)(2,1)}, bf16[512,1024]{1,0:T(8,128)(2,1)}, u32[]{:S(2)}, u32[]{:S(2)}) collective-permute-start(bf16[512,1024]{1,0:T(8,128)(2,1)} %param.19), channel_id=1, source_target_pairs={{0,1},{1,0},{2,3},{3,2},{4,5},{5,4},{6,7},{7,6},{8,9},{9,8},{10,11... | collective-permute-start | bytes 3145736 | tf_op jit(solution)/shard_map/ppermute | solution.py:145
  89.7 26.1 %collective-permute-start.8 = (bf16[512,1024]{1,0:T(8,128)(2,1)S(1)}, bf16[512,1024]{1,0:T(8,128)(2,1)S(1)}, u32[]{:S(2)}, u32[]{:S(2)}) collective-permute-start(bf16[512,1024]{1,0:T(8,128)(2,1)S(1)} %multiply_convert_fusion.6), channel_id=1, source_target_pairs={{0,2},{1,3},{2,0},{3,1},{4,6},{5,7},{6,4},{7,5},{8,10},{9,11},{10,... | collective-permute-start | bytes 3145736 | tf_op jit(solution)/shard_map/ppermute | solution.py:145
  115.9 31.4 %collective-permute-start.14 = (bf16[512,1024]{1,0:T(8,128)(2,1)}, bf16[512,1024]{1,0:T(8,128)(2,1)S(1)}, u32[]{:S(2)}, u32[]{:S(2)}) collective-permute-start(bf16[512,1024]{1,0:T(8,128)(2,1)} %param.19), channel_id=1, source_target_pairs={{0,2},{1,3},{2,0},{3,1},{4,6},{5,7},{6,4},{7,5},{8,10},{9,11},{10,... | collective-permute-start | bytes 3145736 | tf_op jit(solution)/shard_map/ppermute | solution.py:145
  121.8 98.3 %collective-permute-start.13 = (bf16[512,1024]{1,0:T(8,128)(2,1)S(1)}, bf16[512,1024]{1,0:T(8,128)(2,1)S(1)}, u32[]{:S(2)}, u32[]{:S(2)}) collective-permute-start(bf16[512,1024]{1,0:T(8,128)(2,1)S(1)} %constant_dynamic-slice_fusion.19), channel_id=1, source_target_pairs={{0,1},{1,0},{2,3},{3,2},{4,5},{5,4},{6,7},{7,6},{8,9},{9,8},{10,11... | collective-permute-start | bytes 3145736 | tf_op jit(solution)/shard_map/ppermute | solution.py:145
  122.0 22.0 %collective-permute-start.9 = (bf16[512,1024]{1,0:T(8,128)(2,1)S(1)}, bf16[512,1024]{1,0:T(8,128)(2,1)S(1)}, u32[]{:S(2)}, u32[]{:S(2)}) collective-permute-start(bf16[512,1024]{1,0:T(8,128)(2,1)S(1)} %collective-permute-done.8), channel_id=1, source_target_pairs={{0,1},{1,0},{2,3},{3,2},{4,5},{5,4},{6,7},{7,6},{8,9},{9,8},{10,11... | collective-permute-start | bytes 3145736 | tf_op jit(solution)/shard_map/ppermute | solution.py:145
  155.0 38.7 %collective-permute-start.11 = (bf16[512,1024]{1,0:T(8,128)(2,1)S(1)}, bf16[512,1024]{1,0:T(8,128)(2,1)S(1)}, u32[]{:S(2)}, u32[]{:S(2)}) collective-permute-start(bf16[512,1024]{1,0:T(8,128)(2,1)S(1)} %constant_dynamic-slice_fusion.20), channel_id=1, source_target_pairs={{0,1},{1,0},{2,3},{3,2},{4,5},{5,4},{6,7},{7,6},{8,9},{9,8},{10,11... | collective-permute-start | bytes 3145736 | tf_op jit(solution)/shard_map/ppermute | solution.py:145
  176.4 15.8 %collective-permute-start.16 = (bf16[512,1024]{1,0:T(8,128)(2,1)S(1)}, bf16[512,1024]{1,0:T(8,128)(2,1)S(1)}, u32[]{:S(2)}, u32[]{:S(2)}) collective-permute-start(bf16[512,1024]{1,0:T(8,128)(2,1)S(1)} %constant_dynamic-slice_fusion.18), channel_id=1, source_target_pairs={{0,1},{1,0},{2,3},{3,2},{4,5},{5,4},{6,7},{7,6},{8,9},{9,8},{10,11... | collective-permute-start | bytes 3145736 | tf_op jit(solution)/shard_map/ppermute | solution.py:145
  176.6 28.2 %collective-permute-start.59 = (bf16[320,1024]{1,0:T(8,128)(2,1)S(1)}, bf16[320,1024]{1,0:T(8,128)(2,1)S(1)}, u32[]{:S(2)}, u32[]{:S(2)}) collective-permute-start(bf16[320,1024]{1,0:T(8,128)(2,1)S(1)} %constant_dynamic-slice_fusion.3), channel_id=1, source_target_pairs={{0,4},{4,0},{8,12},{12,8},{16,20},{20,16},{24,28},{28,24},{1,5},{5... | collective-permute-start | bytes 1966088 | tf_op jit(solution)/shard_map/ppermute | solution.py:145
  192.7 26.1 %collective-permute-start.17 = (bf16[512,1024]{1,0:T(8,128)(2,1)S(1)}, bf16[512,1024]{1,0:T(8,128)(2,1)S(1)}, u32[]{:S(2)}, u32[]{:S(2)}) collective-permute-start(bf16[512,1024]{1,0:T(8,128)(2,1)S(1)} %add_convert_fusion.7), channel_id=1, source_target_pairs={{0,2},{1,3},{2,0},{3,1},{4,6},{5,7},{6,4},{7,5},{8,10},{9,11},{10,... | collective-permute-start | bytes 3145736 | tf_op jit(solution)/shard_map/ppermute | solution.py:145
  193.8 27.9 %collective-permute-start.7 = (bf16[512,1024]{1,0:T(8,128)(2,1)S(1)}, bf16[512,1024]{1,0:T(8,128)(2,1)S(1)}, u32[]{:S(2)}, u32[]{:S(2)}) collective-permute-start(bf16[512,1024]{1,0:T(8,128)(2,1)S(1)} %constant_dynamic-slice_fusion.21), channel_id=1, source_target_pairs={{0,1},{1,0},{2,3},{3,2},{4,5},{5,4},{6,7},{7,6},{8,9},{9,8},{10,11... | collective-permute-start | bytes 3145736 | tf_op jit(solution)/shard_map/ppermute | solution.py:145
  203.7 36.5 %collective-permute-start.12 = (bf16[512,1024]{1,0:T(8,128)(2,1)S(1)}, bf16[512,1024]{1,0:T(8,128)(2,1)S(1)}, u32[]{:S(2)}, u32[]{:S(2)}) collective-permute-start(bf16[512,1024]{1,0:T(8,128)(2,1)S(1)} %add_convert_fusion.8), channel_id=1, source_target_pairs={{0,2},{1,3},{2,0},{3,1},{4,6},{5,7},{6,4},{7,5},{8,10},{9,11},{10,... | collective-permute-start | bytes 3145736 | tf_op jit(solution)/shard_map/ppermute | solution.py:145
  204.7 104.6 %collective-permute-start.50 = (bf16[192,1152]{1,0:T(8,128)(2,1)}, bf16[192,1152]{1,0:T(8,128)(2,1)}, u32[]{:S(2)}, u32[]{:S(2)}) collective-permute-start(bf16[192,1152]{1,0:T(8,128)(2,1)} %constant_dynamic-slice_fusion.6), channel_id=1, source_target_pairs={{0,8},{4,12},{8,0},{12,4},{16,24},{20,28},{24,16},{28,20},{1,9},{5... | collective-permute-start | bytes 1327112 | tf_op jit(solution)/shard_map/ppermute | solution.py:145
  218.8 90.6 %collective-permute-start.49 = (bf16[320,1152]{1,0:T(8,128)(2,1)}, bf16[320,1152]{1,0:T(8,128)(2,1)S(1)}, u32[]{:S(2)}, u32[]{:S(2)}) collective-permute-start(bf16[320,1152]{1,0:T(8,128)(2,1)} %constant_dynamic-slice_fusion.7), channel_id=1, source_target_pairs={{0,4},{4,0},{8,12},{12,8},{16,20},{20,16},{24,28},{28,24},{1,5},{5... | collective-permute-start | bytes 2211848 | tf_op jit(solution)/shard_map/ppermute | solution.py:145
  220.1 45.8 %collective-permute-start.39 = (bf16[320,1152]{1,0:T(8,128)(2,1)S(1)}, bf16[320,1152]{1,0:T(8,128)(2,1)S(1)}, u32[]{:S(2)}, u32[]{:S(2)}) collective-permute-start(bf16[320,1152]{1,0:T(8,128)(2,1)S(1)} %constant_dynamic-slice_fusion.11), channel_id=1, source_target_pairs={{0,4},{4,0},{8,12},{12,8},{16,20},{20,16},{24,28},{28,24},{1,5},{5... | collective-permute-start | bytes 2211848 | tf_op jit(solution)/shard_map/ppermute | solution.py:145
  221.7 35.1 %collective-permute-start.62 = (bf16[128,1024]{1,0:T(8,128)(2,1)S(1)}, bf16[128,1024]{1,0:T(8,128)(2,1)S(1)}, u32[]{:S(2)}, u32[]{:S(2)}) collective-permute-start(bf16[128,1024]{1,0:T(8,128)(2,1)S(1)} %constant_dynamic-slice_fusion), channel_id=1, source_target_pairs={{0,4},{4,0},{8,12},{12,8},{16,20},{20,16},{24,28},{28,24},{1,5},{5... | collective-permute-start | bytes 786440 | tf_op jit(solution)/shard_map/ppermute | solution.py:145
  240.2 17.2 %collective-permute-start.61 = (bf16[160,1024]{1,0:T(8,128)(2,1)S(1)}, bf16[160,1024]{1,0:T(8,128)(2,1)S(1)}, u32[]{:S(2)}, u32[]{:S(2)}) collective-permute-start(bf16[160,1024]{1,0:T(8,128)(2,1)S(1)} %constant_dynamic-slice_fusion.1), channel_id=1, source_target_pairs={{0,8},{4,12},{8,0},{12,4},{16,24},{20,28},{24,16},{28,20},{1,9},{5... | collective-permute-start | bytes 983048 | tf_op jit(solution)/shard_map/ppermute | solution.py:145
  257.4 22.0 %collective-permute-start.20 = (bf16[512,1024]{1,0:T(8,128)(2,1)S(1)}, bf16[512,1024]{1,0:T(8,128)(2,1)S(1)}, u32[]{:S(2)}, u32[]{:S(2)}) collective-permute-start(bf16[512,1024]{1,0:T(8,128)(2,1)S(1)} %get-tuple-element.102), channel_id=1, source_target_pairs={{0,2},{1,3},{2,0},{3,1},{4,6},{5,7},{6,4},{7,5},{8,10},{9,11},{10,... | collective-permute-start | bytes 3145736 | tf_op jit(solution)/shard_map/ppermute | solution.py:145
  265.9 14.1 %collective-permute-start.18 = (bf16[512,1024]{1,0:T(8,128)(2,1)S(1)}, bf16[512,1024]{1,0:T(8,128)(2,1)S(1)}, u32[]{:S(2)}, u32[]{:S(2)}) collective-permute-start(bf16[512,1024]{1,0:T(8,128)(2,1)S(1)} %get-tuple-element.102), channel_id=1, source_target_pairs={{0,1},{1,0},{2,3},{3,2},{4,5},{5,4},{6,7},{7,6},{8,9},{9,8},{10,11... | collective-permute-start | bytes 3145736 | tf_op jit(solution)/shard_map/ppermute | solution.py:145
  266.0 31.1 %collective-permute-start.63 = (bf16[144,1024]{1,0:T(8,128)(2,1)S(1)}, bf16[144,1024]{1,0:T(8,128)(2,1)S(1)}, u32[]{:S(2)}, u32[]{:S(2)}) collective-permute-start(bf16[144,1024]{1,0:T(8,128)(2,1)S(1)} %fusion.34), channel_id=1, source_target_pairs={{0,16},{4,20},{8,24},{12,28},{16,0},{20,4},{24,8},{28,12},{1,17},{... | collective-permute-start | bytes 884744 | tf_op jit(solution)/shard_map/ppermute | solution.py:145
  280.1 109.7 %collective-permute-start.42 = (bf16[96,1152]{1,0:T(8,128)(2,1)}, bf16[96,1152]{1,0:T(8,128)(2,1)}, u32[]{:S(2)}, u32[]{:S(2)}) collective-permute-start(bf16[96,1152]{1,0:T(8,128)(2,1)} %constant_dynamic-slice_fusion.8), channel_id=1, source_target_pairs={{0,4},{4,0},{8,12},{12,8},{16,20},{20,16},{24,28},{28,24},{1,5},{5... | collective-permute-start | bytes 663560 | tf_op jit(solution)/shard_map/ppermute | solution.py:145
  284.8 108.3 %collective-permute-start.41 = (bf16[160,1152]{1,0:T(8,128)(2,1)}, bf16[160,1152]{1,0:T(8,128)(2,1)}, u32[]{:S(2)}, u32[]{:S(2)}) collective-permute-start(bf16[160,1152]{1,0:T(8,128)(2,1)} %constant_dynamic-slice_fusion.9), channel_id=1, source_target_pairs={{0,8},{4,12},{8,0},{12,4},{16,24},{20,28},{24,16},{28,20},{1,9},{5... | collective-permute-start | bytes 1105928 | tf_op jit(solution)/shard_map/ppermute | solution.py:145
  303.6 85.1 %collective-permute-start.64 = (bf16[144,1024]{1,0:T(8,128)(2,1)}, bf16[144,1024]{1,0:T(8,128)(2,1)}, u32[]{:S(2)}, u32[]{:S(2)}) collective-permute-start(bf16[144,1024]{1,0:T(8,128)(2,1)} %add_convert_fusion.22), channel_id=1, source_target_pairs={{0,16},{4,20},{8,24},{12,28},{16,0},{20,4},{24,8},{28,12},{1,17},{... | collective-permute-start | bytes 884744 | tf_op jit(solution)/shard_map/ppermute | solution.py:145
  314.3 14.2 %collective-permute-start.51 = (bf16[160,1152]{1,0:T(8,128)(2,1)}, bf16[160,1152]{1,0:T(8,128)(2,1)}, u32[]{:S(2)}, u32[]{:S(2)}) collective-permute-start(bf16[160,1152]{1,0:T(8,128)(2,1)} %constant_dynamic-slice_fusion.5), channel_id=1, source_target_pairs={{0,8},{4,12},{8,0},{12,4},{16,24},{20,28},{24,16},{28,20},{1,9},{5... | collective-permute-start | bytes 1105928 | tf_op jit(solution)/shard_map/ppermute | solution.py:145
  319.2 26.6 %collective-permute-start.24 = (bf16[320,1024]{1,0:T(8,128)(2,1)S(1)}, bf16[320,1024]{1,0:T(8,128)(2,1)S(1)}, u32[]{:S(2)}, u32[]{:S(2)}) collective-permute-start(bf16[320,1024]{1,0:T(8,128)(2,1)S(1)} %constant_dynamic-slice_fusion.15), channel_id=1, source_target_pairs={{0,4},{4,0},{8,12},{12,8},{16,20},{20,16},{24,28},{28,24},{1,5},{5... | collective-permute-start | bytes 1966088 | tf_op jit(solution)/shard_map/ppermute | solution.py:145
  345.7 41.8 %collective-permute-start.22 = (bf16[512,1024]{1,0:T(8,128)(2,1)S(1)}, bf16[512,1024]{1,0:T(8,128)(2,1)S(1)}, u32[]{:S(2)}, u32[]{:S(2)}) collective-permute-start(bf16[512,1024]{1,0:T(8,128)(2,1)S(1)} %constant_dynamic-slice_fusion.16), channel_id=1, source_target_pairs={{0,1},{1,0},{2,3},{3,2},{4,5},{5,4},{6,7},{7,6},{8,9},{9,8},{10,11... | collective-permute-start | bytes 3145736 | tf_op jit(solution)/shard_map/ppermute | solution.py:145
  345.8 16.7 %collective-permute-start.53 = (bf16[128,1152]{1,0:T(8,128)(2,1)S(1)}, bf16[128,1152]{1,0:T(8,128)(2,1)S(1)}, u32[]{:S(2)}, u32[]{:S(2)}) collective-permute-start(bf16[128,1152]{1,0:T(8,128)(2,1)S(1)} %fusion.30), channel_id=1, source_target_pairs={{0,16},{4,20},{8,24},{12,28},{16,0},{20,4},{24,8},{28,12},{1,17},{... | collective-permute-start | bytes 884744 | tf_op jit(solution)/shard_map/ppermute | solution.py:145
  371.9 15.4 %collective-permute-start.54 = (bf16[128,1152]{1,0:T(8,128)(2,1)S(1)}, bf16[128,1152]{1,0:T(8,128)(2,1)S(1)}, u32[]{:S(2)}, u32[]{:S(2)}) collective-permute-start(bf16[128,1152]{1,0:T(8,128)(2,1)S(1)} %add_convert_fusion.23), channel_id=1, source_target_pairs={{0,16},{4,20},{8,24},{12,28},{16,0},{20,4},{24,8},{28,12},{1,17},{... | collective-permute-start | bytes 884744 | tf_op jit(solution)/shard_map/ppermute | solution.py:145
  387.2 113.4 %collective-permute-start.19 = (bf16[512,1024]{1,0:T(8,128)(2,1)S(1)}, bf16[512,1024]{1,0:T(8,128)(2,1)S(1)}, u32[]{:S(2)}, u32[]{:S(2)}) collective-permute-start(bf16[512,1024]{1,0:T(8,128)(2,1)S(1)} %copy-done.54), channel_id=1, source_target_pairs={{0,1},{1,0},{2,3},{3,2},{4,5},{5,4},{6,7},{7,6},{8,9},{9,8},{10,11... | collective-permute-start | bytes 3145736 | tf_op jit(solution)/shard_map/ppermute | solution.py:145
  387.6 31.6 %collective-permute-start.55 = (bf16[160,1152]{1,0:T(8,128)(2,1)S(1)}, bf16[160,1152]{1,0:T(8,128)(2,1)S(1)}, u32[]{:S(2)}, u32[]{:S(2)}) collective-permute-start(bf16[160,1152]{1,0:T(8,128)(2,1)S(1)} %pad_maximum_fusion.36), channel_id=1, source_target_pairs={{0,8},{4,12},{8,0},{12,4},{16,24},{20,28},{24,16},{28,20},{1,9},{5... | collective-permute-start | bytes 1105928 | tf_op jit(solution)/shard_map/ppermute | solution.py:145
  388.7 29.3 %collective-permute-start.56 = (bf16[96,1152]{1,0:T(8,128)(2,1)S(1)}, bf16[96,1152]{1,0:T(8,128)(2,1)S(1)}, u32[]{:S(2)}, u32[]{:S(2)}) collective-permute-start(bf16[96,1152]{1,0:T(8,128)(2,1)S(1)} %slice.197), channel_id=1, source_target_pairs={{0,4},{4,0},{8,12},{12,8},{16,20},{20,16},{24,28},{28,24},{1,5},{5... | collective-permute-start | bytes 663560 | tf_op jit(solution)/shard_map/ppermute | solution.py:145
  395.4 22.4 %collective-permute-start.43 = (bf16[128,1152]{1,0:T(8,128)(2,1)S(1)}, bf16[128,1152]{1,0:T(8,128)(2,1)S(1)}, u32[]{:S(2)}, u32[]{:S(2)}) collective-permute-start(bf16[128,1152]{1,0:T(8,128)(2,1)S(1)} %fusion.32), channel_id=1, source_target_pairs={{0,16},{4,20},{8,24},{12,28},{16,0},{20,4},{24,8},{28,12},{1,17},{... | collective-permute-start | bytes 884744 | tf_op jit(solution)/shard_map/ppermute | solution.py:145
  402.9 98.4 %collective-permute-start.23 = (bf16[512,1024]{1,0:T(8,128)(2,1)S(1)}, bf16[512,1024]{1,0:T(8,128)(2,1)S(1)}, u32[]{:S(2)}, u32[]{:S(2)}) collective-permute-start(bf16[512,1024]{1,0:T(8,128)(2,1)S(1)} %add_convert_fusion.6), channel_id=1, source_target_pairs={{0,2},{1,3},{2,0},{3,1},{4,6},{5,7},{6,4},{7,5},{8,10},{9,11},{10,... | collective-permute-start | bytes 3145736 | tf_op jit(solution)/shard_map/ppermute | solution.py:145
  417.8 14.7 %collective-permute-start.65 = (bf16[160,1024]{1,0:T(8,128)(2,1)S(1)}, bf16[160,1024]{1,0:T(8,128)(2,1)S(1)}, u32[]{:S(2)}, u32[]{:S(2)}) collective-permute-start(bf16[160,1024]{1,0:T(8,128)(2,1)S(1)} %pad_maximum_fusion.38), channel_id=1, source_target_pairs={{0,8},{4,12},{8,0},{12,4},{16,24},{20,28},{24,16},{28,20},{1,9},{5... | collective-permute-start | bytes 983048 | tf_op jit(solution)/shard_map/ppermute | solution.py:145
  419.2 20.0 %collective-permute-start.29 = (bf16[128,1024]{1,0:T(8,128)(2,1)S(1)}, bf16[128,1024]{1,0:T(8,128)(2,1)S(1)}, u32[]{:S(2)}, u32[]{:S(2)}) collective-permute-start(bf16[128,1024]{1,0:T(8,128)(2,1)S(1)} %add_convert_fusion.26), channel_id=1, source_target_pairs={{0,16},{4,20},{8,24},{12,28},{16,0},{20,4},{24,8},{28,12},{1,17},{... | collective-permute-start | bytes 786440 | tf_op jit(solution)/shard_map/ppermute | solution.py:145
  425.7 20.2 %collective-permute-start.44 = (bf16[128,1152]{1,0:T(8,128)(2,1)S(1)}, bf16[128,1152]{1,0:T(8,128)(2,1)S(1)}, u32[]{:S(2)}, u32[]{:S(2)}) collective-permute-start(bf16[128,1152]{1,0:T(8,128)(2,1)S(1)} %add_convert_fusion.24), channel_id=1, source_target_pairs={{0,16},{4,20},{8,24},{12,28},{16,0},{20,4},{24,8},{28,12},{1,17},{... | collective-permute-start | bytes 884744 | tf_op jit(solution)/shard_map/ppermute | solution.py:145
  432.5 71.8 %collective-permute-start.57 = (bf16[320,1152]{1,0:T(8,128)(2,1)S(1)}, bf16[320,1152]{1,0:T(8,128)(2,1)S(1)}, u32[]{:S(2)}, u32[]{:S(2)}) collective-permute-start(bf16[320,1152]{1,0:T(8,128)(2,1)S(1)} %pad_maximum_fusion.24), channel_id=1, source_target_pairs={{0,4},{4,0},{8,12},{12,8},{16,20},{20,16},{24,28},{28,24},{1,5},{5... | collective-permute-start | bytes 2211848 | tf_op jit(solution)/shard_map/ppermute | solution.py:145
  439.2 14.5 %collective-permute-start.58 = (bf16[192,1152]{1,0:T(8,128)(2,1)S(1)}, bf16[192,1152]{1,0:T(8,128)(2,1)S(1)}, u32[]{:S(2)}, u32[]{:S(2)}) collective-permute-start(bf16[192,1152]{1,0:T(8,128)(2,1)S(1)} %pad_maximum_fusion.34), channel_id=1, source_target_pairs={{0,8},{4,12},{8,0},{12,4},{16,24},{20,28},{24,16},{28,20},{1,9},{5... | collective-permute-start | bytes 1327112 | tf_op jit(solution)/shard_map/ppermute | solution.py:145
  453.6 21.6 %collective-permute-start.68 = (bf16[256,1024]{1,0:T(8,128)(2,1)S(1)}, bf16[256,1024]{1,0:T(8,128)(2,1)S(1)}, u32[]{:S(2)}, u32[]{:S(2)}) collective-permute-start(bf16[256,1024]{1,0:T(8,128)(2,1)S(1)} %pad_maximum_fusion.32), channel_id=1, source_target_pairs={{0,8},{4,12},{8,0},{12,4},{16,24},{20,28},{24,16},{28,20},{1,9},{5... | collective-permute-start | bytes 1572872 | tf_op jit(solution)/shard_map/ppermute | solution.py:145
  453.7 19.5 %collective-permute-start.30 = (bf16[160,1024]{1,0:T(8,128)(2,1)S(1)}, bf16[160,1024]{1,0:T(8,128)(2,1)S(1)}, u32[]{:S(2)}, u32[]{:S(2)}) collective-permute-start(bf16[160,1024]{1,0:T(8,128)(2,1)S(1)} %pad_maximum_fusion.39), channel_id=1, source_target_pairs={{0,8},{4,12},{8,0},{12,4},{16,24},{20,28},{24,16},{28,20},{1,9},{5... | collective-permute-start | bytes 983048 | tf_op jit(solution)/shard_map/ppermute | solution.py:145
  481.5 14.7 %collective-permute-start.67 = (bf16[320,1024]{1,0:T(8,128)(2,1)S(1)}, bf16[320,1024]{1,0:T(8,128)(2,1)S(1)}, u32[]{:S(2)}, u32[]{:S(2)}) collective-permute-start(bf16[320,1024]{1,0:T(8,128)(2,1)S(1)} %pad_maximum_fusion.27), channel_id=1, source_target_pairs={{0,4},{4,0},{8,12},{12,8},{16,20},{20,16},{24,28},{28,24},{1,5},{5... | collective-permute-start | bytes 1966088 | tf_op jit(solution)/shard_map/ppermute | solution.py:145
  482.8 48.2 %collective-permute-start.33 = (bf16[192,1024]{1,0:T(8,128)(2,1)S(1)}, bf16[192,1024]{1,0:T(8,128)(2,1)S(1)}, u32[]{:S(2)}, u32[]{:S(2)}) collective-permute-start(bf16[192,1024]{1,0:T(8,128)(2,1)S(1)} %pad_maximum_fusion.35), channel_id=1, source_target_pairs={{0,8},{4,12},{8,0},{12,4},{16,24},{20,28},{24,16},{28,20},{1,9},{5... | collective-permute-start | bytes 1179656 | tf_op jit(solution)/shard_map/ppermute | solution.py:145
  496.2 41.1 %collective-permute-start.31 = (bf16[320,1024]{1,0:T(8,128)(2,1)}, bf16[320,1024]{1,0:T(8,128)(2,1)}, u32[]{:S(2)}, u32[]{:S(2)}) collective-permute-start(bf16[320,1024]{1,0:T(8,128)(2,1)} %pad_maximum_fusion.26), channel_id=1, source_target_pairs={{0,4},{4,0},{8,12},{12,8},{16,20},{20,16},{24,28},{28,24},{1,5},{5... | collective-permute-start | bytes 1966088 | tf_op jit(solution)/shard_map/ppermute | solution.py:145
  500.6 46.3 %collective-permute-start.47 = (bf16[320,1152]{1,0:T(8,128)(2,1)}, bf16[320,1152]{1,0:T(8,128)(2,1)}, u32[]{:S(2)}, u32[]{:S(2)}) collective-permute-start(bf16[320,1152]{1,0:T(8,128)(2,1)} %pad_maximum_fusion.23), channel_id=1, source_target_pairs={{0,4},{4,0},{8,12},{12,8},{16,20},{20,16},{24,28},{28,24},{1,5},{5... | collective-permute-start | bytes 2211848 | tf_op jit(solution)/shard_map/ppermute | solution.py:145
  501.3 33.8 %collective-permute-start.48 = (bf16[192,1152]{1,0:T(8,128)(2,1)}, bf16[192,1152]{1,0:T(8,128)(2,1)}, u32[]{:S(2)}, u32[]{:S(2)}) collective-permute-start(bf16[192,1152]{1,0:T(8,128)(2,1)} %pad_maximum_fusion.33), channel_id=1, source_target_pairs={{0,8},{4,12},{8,0},{12,4},{16,24},{20,28},{24,16},{28,20},{1,9},{5... | collective-permute-start | bytes 1327112 | tf_op jit(solution)/shard_map/ppermute | solution.py:145
  509.3 15.9 %collective-permute-start.36 = (f32[2816]{0:T(1024)S(1)}, f32[2816]{0:T(1024)S(1)}, u32[]{:S(2)}, u32[]{:S(2)}) collective-permute-start(f32[2816]{0:T(1024)S(1)} %constant_dynamic-update-slice_fusion), channel_id=1, source_target_pairs={{0,4},{4,0},{8,12},{12,8},{16,20},{20,16},{24,28},{28,24},{1,5},{5... | collective-permute-start | bytes 33800 | tf_op jit(solution)/shard_map/ppermute | solution.py:145
  (100 other events, 799.4 us)
